TPU v7x, 256 devices: a whole 4x4x8 slice. The times are simulated.
256 devices in a mesh: dp: 4 (over x), group: 2 (over core), expert: 32 (over y, z).
Axes of the slice: x: 4, y: 4, z: 8, core: 2. Of those that a mesh axis runs over, the one named last changes fastest.
Arguments:
- tokens: bfloat16 [8192, 3584], P(('group', 'expert')), may hold values from -6 to 6
- expert_ids: int32 [8192, 2], P(('group', 'expert')), may hold values from 0 to 31, all different within a row; in each aligned block of 128 rows (0 to 127, 128 to 255, ...) at most 10 rows name the same one
- gates: float32 [8192, 2], P(('group', 'expert')), may hold values from 0.1 to 1
- w_gate: bfloat16 [32, 3584, 3072], P('expert', None, ('dp', 'group')), may hold values from -0.09375 to 0.09375
- w_up: bfloat16 [32, 3584, 3072], P('expert', None, ('dp', 'group')), may hold values from -0.09375 to 0.09375
- w_down: bfloat16 [32, 3072, 3584], P('expert', ('dp', 'group')), may hold values from -0.109375 to 0.109375
- cotangent: bfloat16 [8192, 3584], P(('group', 'expert'), 'dp'), may hold values from -1.1953125 to 1.1953125
Outputs:
- mixed: bfloat16 [8192, 3584], P(('group', 'expert'), 'dp')
- d_tokens: bfloat16 [8192, 3584], P(('group', 'expert'), 'dp')
- d_gates: float32 [8192, 2], P(('group', 'expert'))
Inputs may be any that keep to these rules, and one draw needn't show every extreme that they name: `expert_ids`: the two experts of a token differ. Within each aligned block of 128 tokens no expert is named by more than 10 tokens, a bound that some block reaches.
All inputs are finite; a program needn't handle non-finite values.
Results may differ from a plain program's by a relative error of at most 0.012.
Values may be sent and summed in bfloat16 or wider, within the bound.
No kernel may reach another device: no remote copies, remote signals or barrier semaphores. Data moves between devices by JAX's collectives and lax.ppermute only.
A program may use at most 128 MiB of HBM per device.

v0:
```python
import functools
import jax
import jax.numpy as jnp
from jax import lax
from jax.experimental import pallas as pl
from jax.experimental.pallas import tpu as pltpu
from jax.sharding import PartitionSpec as P

BF = jnp.bfloat16
F32 = jnp.float32
TOK = 128
EXP = 32
MAIN = 8
OVER = 2
LANE = 128
NDP = 4
D = 3584
QD = D // NDP
CH = QD // LANE
ROWS = EXP * MAIN
WIDE = QD + OVER * LANE
ALL = ROWS + EXP * OVER
HALF = ROWS // 2
HD = 384
VMEM = 24 * 1024 * 1024
COST = pl.CostEstimate(flops=1000, bytes_accessed=1000, transcendentals=0)
LONG_COST = pl.CostEstimate(flops=6_000_000_000, bytes_accessed=1000, transcendentals=0)
NT = (((1,), (1,)), ((), ()))
TN = (((0,), (0,)), ((), ()))


def hbm(x):
    return pltpu.with_memory_space_constraint(x, pltpu.HBM)


def params():
    return pltpu.CompilerParams(vmem_limit_bytes=VMEM)


def iota(shape, dim):
    return lax.broadcasted_iota(jnp.int32, shape, dim)


def dot(a, b, dims=(((1,), (0,)), ((), ()))):
    return lax.dot_general(a, b, dims, preferred_element_type=F32)


def spread(flip):
    shape = (CH * EXP, ROWS) if flip else (ROWS, CH * EXP)
    row, col = iota(shape, int(flip)), iota(shape, 1 - int(flip))
    return ((row % MAIN == col // EXP) & (row // MAIN == col % EXP)).astype(F32).astype(BF)


def pack(over):
    parts = [
        jnp.concatenate([over[c * EXP:(c + 1) * EXP, r * LANE:(r + 1) * LANE] for c in range(OVER)], axis=1)
        for r in range(CH)
    ]
    return dot(spread(False), jnp.concatenate(parts, axis=0)).astype(BF)


def unpack(packed):
    rows = dot(spread(True), packed).astype(BF)
    parts = [
        jnp.concatenate([rows[r * EXP:(r + 1) * EXP, c * LANE:(c + 1) * LANE] for c in range(OVER)], axis=0)
        for r in range(CH)
    ]
    return jnp.concatenate(parts, axis=1)


def join(piece):
    return jnp.concatenate([piece[:, :QD], unpack(piece[:, QD:])], axis=0)


def split(rows):
    return jnp.concatenate([rows[:ROWS], pack(rows[ROWS:])], axis=1)


def columns(rows):
    return [jnp.broadcast_to(rows[k:k + 1], (TOK, TOK)).T for k in range(2)]


def choose(ids):
    lane = iota((TOK, EXP), 1).astype(F32)
    cols = columns(ids.astype(F32))
    hot = [(col[:, :EXP] == lane).astype(F32) for col in cols]
    lower = (iota((TOK, TOK), 1) < iota((TOK, TOK), 0)).astype(F32).astype(BF)
    earlier = dot(lower, (hot[0] + hot[1]).astype(BF))
    out = []
    for k in range(2):
        slot = jnp.sum(earlier * hot[k], axis=1, keepdims=True)
        e = cols[k][:, :1]
        dest = jnp.where(slot < MAIN, e * MAIN + slot, ROWS + (slot - MAIN) * EXP + e).astype(jnp.int32)
        out.append((iota((TOK, ALL), 1) == dest).astype(F32).astype(BF))
    return out


def pack_kernel(d_ref, ids_ref, gates_ref, tok_ref, cot_ref, x_ref, z_ref):
    m0, m1 = choose(ids_ref[...])
    gate = [col[:, :1] for col in columns(gates_ref[...])]
    cot = cot_ref[...].astype(F32)
    x_ref[...] = split(dot(m0 + m1, tok_ref[...], TN).astype(BF))
    z0 = (gate[0] * cot).astype(BF)
    z1 = (gate[1] * cot).astype(BF)
    z_ref[...] = split((dot(m0, z0, TN) + dot(m1, z1, TN)).astype(BF))


def pack_call(d, ids, gates, tokens, cot):
    full = lambda shape: pl.BlockSpec(shape, lambda i, d_ref: (0, 0))
    shape = jax.ShapeDtypeStruct((ROWS, WIDE), BF)
    return pl.pallas_call(
        pack_kernel,
        grid_spec=pltpu.PrefetchScalarGridSpec(
            num_scalar_prefetch=1,
            grid=(1,),
            in_specs=[
                full((2, TOK)),
                full((2, TOK)),
                pl.BlockSpec((TOK, QD), lambda i, d_ref: (0, d_ref[0])),
                full((TOK, QD)),
            ],
            out_specs=[full((ROWS, WIDE))] * 2,
        ),
        out_shape=[shape, shape],
        compiler_params=params(),
        cost_estimate=COST,
    )(d, ids, gates, hbm(tokens), hbm(cot))


def part_of(d, j):
    return pl.ds(pl.multiple_of(((d + j) % NDP) * QD, QD), QD)


NEAR = (0, 1, 3)
FAR = (2,)
IN_W = (QD, 2 * HD)
DOWN_W = (2 * HD, QD)


def fetch(d, pair, buf, sems, pieces, down, i):
    copies = []
    for c, w in enumerate(pair):
        own = pl.ds(c * HD, HD)
        if down:
            src, dst = w.at[:, part_of(d, pieces[i])], buf.at[i, own, :]
        else:
            src, dst = w.at[part_of(d, pieces[i]), :], buf.at[i, :, own]
        copies.append(pltpu.make_async_copy(src, dst, sems.at[i, c]))
        copies[-1].start()
    return copies


def bring(piece, buf, sems, i):
    copy = pltpu.make_async_copy(piece, buf.at[i], sems.at[i])
    copy.start()
    return [copy]


def wait_for(copies):
    for copy in copies:
        copy.wait()


def fwd_near_kernel(
    d_ref, own, high, low, wg0, wg1, wu0, wu1, a_ref, b_ref, gate, up, slots, gate_sem, up_sem, slot_sem
):
    d = d_ref[0]
    copies = []
    for i, piece in enumerate((own, high, low)):
        copies.append((
            bring(piece, slots, slot_sem, i),
            fetch(d, (wg0, wg1), gate, gate_sem, NEAR, False, i),
            fetch(d, (wu0, wu1), up, up_sem, NEAR, False, i),
        ))
    for i, (slot, *both) in enumerate(copies):
        wait_for(slot)
        rows = join(slots[i])
        for out, weights, buf in ((a_ref, both[0], gate), (b_ref, both[1], up)):
            wait_for(weights)
            part = dot(rows, buf[i])
            out[...] = part if i == 0 else out[...] + part


def fwd_far_kernel(
    d_ref, far_a, far_b, a_in, b_in, wg0, wg1, wu0, wu1, wd0, wd1,
    a_ref, b_ref, h_ref, out_a, out_b, gate, up, down, gate_sem, up_sem, down_sem,
):
    d = d_ref[0]
    gates = fetch(d, (wg0, wg1), gate, gate_sem, FAR, False, 0)
    ups = fetch(d, (wu0, wu1), up, up_sem, FAR, False, 0)
    downs = fetch(d, (wd0, wd1), down, down_sem, FAR, True, 0)
    rows = join(jnp.concatenate([far_a[...], far_b[...]], axis=0))
    wait_for(gates)
    a_ref[...] = a_in[...] + dot(rows, gate[0])
    wait_for(ups)
    b_ref[...] = b_in[...] + dot(rows, up[0])
    a, b = a_ref[...], b_ref[...]
    h_ref[...] = (a * jax.nn.sigmoid(a) * b).astype(BF)
    wait_for(downs)
    out = split(dot(h_ref[...], down[0]).astype(BF))
    out_a[...] = out[:HALF]
    out_b[...] = out[HALF:]


def fwd_rest_kernel(d_ref, h_ref, wd0, wd1, own, high, low, down, down_sem):
    downs = [fetch(d_ref[0], (wd0, wd1), down, down_sem, NEAR, True, i) for i in range(len(NEAR))]
    for i, ref in enumerate((own, high, low)):
        wait_for(downs[i])
        ref[...] = split(dot(h_ref[...], down[i]).astype(BF))


def bwd_near_kernel(d_ref, own, high, low, wd0, wd1, g_ref, down, slots, down_sem, slot_sem):
    copies = []
    for i, piece in enumerate((own, high, low)):
        copies.append((
            bring(piece, slots, slot_sem, i),
            fetch(d_ref[0], (wd0, wd1), down, down_sem, NEAR, True, i),
        ))
    for i, (slot, weights) in enumerate(copies):
        wait_for(slot)
        rows = join(slots[i])
        wait_for(weights)
        part = dot(rows, down[i], NT)
        g_ref[...] = part if i == 0 else g_ref[...] + part


def bwd_far_kernel(
    d_ref, far_a, far_b, g_in, a_ref, b_ref, wg0, wg1, wu0, wu1, wd0, wd1,
    da_ref, db_ref, out_a, out_b, gate, up, down, gate_sem, up_sem, down_sem,
):
    d = d_ref[0]
    downs = fetch(d, (wd0, wd1), down, down_sem, FAR, True, 0)
    gates = fetch(d, (wg0, wg1), gate, gate_sem, FAR, False, 0)
    ups = fetch(d, (wu0, wu1), up, up_sem, FAR, False, 0)
    rows = join(jnp.concatenate([far_a[...], far_b[...]], axis=0))
    wait_for(downs)
    g = g_in[...] + dot(rows, down[0], NT)
    a, b = a_ref[...], b_ref[...]
    s = jax.nn.sigmoid(a)
    da_ref[...] = (g * b * s * (1.0 + a * (1.0 - s))).astype(BF)
    db_ref[...] = (g * a * s).astype(BF)
    wait_for(gates)
    wait_for(ups)
    out = split((dot(da_ref[...], gate[0], NT) + dot(db_ref[...], up[0], NT)).astype(BF))
    out_a[...] = out[:HALF]
    out_b[...] = out[HALF:]


def bwd_rest_kernel(d_ref, da_ref, db_ref, wg0, wg1, wu0, wu1, own, high, low, gate, up, gate_sem, up_sem):
    d = d_ref[0]
    copies = [
        fetch(d, (wg0, wg1), gate, gate_sem, NEAR, False, i) + fetch(d, (wu0, wu1), up, up_sem, NEAR, False, i)
        for i in range(len(NEAR))
    ]
    for i, ref in enumerate((own, high, low)):
        wait_for(copies[i])
        ref[...] = split((dot(da_ref[...], gate[i], NT) + dot(db_ref[...], up[i], NT)).astype(BF))


INSIDE = pl.BlockSpec(memory_space=pltpu.VMEM)
OUTSIDE = pl.BlockSpec(memory_space=pltpu.HBM)
HIDDEN = (ALL, 2 * HD)


def expert_call(kernel, d, ins, weights, outs, buffers, pieces, slots=()):
    count = len(pieces)
    space = [pltpu.VMEM((count, *shape), BF) for shape in buffers]
    sems = [pltpu.SemaphoreType.DMA((count, 2)) for _ in buffers]
    if slots:
        space.append(pltpu.VMEM((len(slots), ROWS, WIDE), BF))
        sems.append(pltpu.SemaphoreType.DMA((len(slots),)))
    return pl.pallas_call(
        kernel,
        in_specs=[pl.BlockSpec(memory_space=pltpu.SMEM)]
        + [OUTSIDE] * len(slots) + [INSIDE] * len(ins) + [OUTSIDE] * len(weights),
        out_specs=[INSIDE] * len(outs),
        out_shape=[jax.ShapeDtypeStruct(shape, kind) for shape, kind in outs],
        scratch_shapes=space + sems,
        compiler_params=params(),
        cost_estimate=COST if kernel in (fwd_far_kernel, fwd_rest_kernel, bwd_far_kernel) else LONG_COST,
    )(d, *slots, *ins, *weights)


def halves_kernel(high, low, low_a, high_b, sems):
    copies = [
        pltpu.make_async_copy(low.at[pl.ds(0, HALF), :], low_a, sems.at[0]),
        pltpu.make_async_copy(high.at[pl.ds(HALF, HALF), :], high_b, sems.at[1]),
    ]
    for copy in copies:
        copy.start()
    for copy in copies:
        copy.wait()


def halves_call(high, low):
    return pl.pallas_call(
        halves_kernel,
        in_specs=[OUTSIDE] * 2,
        out_specs=[INSIDE] * 2,
        out_shape=[jax.ShapeDtypeStruct((HALF, WIDE), BF)] * 2,
        scratch_shapes=[pltpu.SemaphoreType.DMA((2,))],
        compiler_params=params(),
        cost_estimate=COST,
    )(high, low)


SLOT_ROWS = ((ROWS, WIDE), BF)
HALF_ROWS = ((HALF, WIDE), BF)
SUMS = (HIDDEN, F32)
UNITS = (HIDDEN, BF)


def mix_kernel(ids_ref, gates_ref, cot_ref, out_ref, mixed_ref, dg_ref):
    hots = choose(ids_ref[...])
    rows = join(out_ref[...])
    gate = [col[:, :1] for col in columns(gates_ref[...])]
    cot = cot_ref[...].astype(F32)
    mixed = jnp.zeros((TOK, QD), F32)
    for k in range(2):
        mine = dot(hots[k], rows)
        mixed = mixed + gate[k] * mine
        dg_ref[:, k:k + 1] = jnp.sum(cot * mine, axis=1, keepdims=True)
    mixed_ref[...] = mixed.astype(BF)


def mix_call(ids, gates, cot, out):
    return pl.pallas_call(
        mix_kernel,
        out_shape=[jax.ShapeDtypeStruct((TOK, QD), BF), jax.ShapeDtypeStruct((TOK, 2), F32)],
        compiler_params=params(),
        cost_estimate=COST,
    )(ids, gates, cot, out)


def dtok_kernel(ids_ref, dx_ref, out_ref):
    m0, m1 = choose(ids_ref[...])
    out_ref[...] = dot(m0 + m1, join(dx_ref[...])).astype(BF)


def dtok_call(ids, dx):
    return pl.pallas_call(
        dtok_kernel,
        out_shape=jax.ShapeDtypeStruct((TOK, QD), BF),
        compiler_params=params(),
        cost_estimate=COST,
    )(ids, dx)


def move(x, by):
    return lax.ppermute(x, "dp", [(i, (i + by) % NDP) for i in range(NDP)])


def gather_near(own):
    return move(own, -1), move(own, 1)


def gather_far(high, low):
    low_a, high_b = halves_call(high, low)
    return move(low_a, 1), move(high_b, -1)


def local_call(kernel, outs, *ins):
    return pl.pallas_call(
        kernel,
        out_shape=[jax.ShapeDtypeStruct(shape, kind) for shape, kind in outs],
        compiler_params=params(),
        cost_estimate=COST,
    )(*ins)


def add(*terms):
    total = terms[0].astype(F32)
    for term in terms[1:]:
        total = total + term.astype(F32)
    return total.astype(BF)


def add_far_kernel(high, low, got_a, got_b, high_out, low_out):
    high_out[:HALF] = add(high[:HALF], got_a[...])
    high_out[HALF:] = high[HALF:]
    low_out[:HALF] = low[:HALF]
    low_out[HALF:] = add(low[HALF:], got_b[...])


def add_near_kernel(own, from_low, from_high, out):
    out[...] = add(own[...], from_low[...], from_high[...])


def reduce_far(far_a, far_b):
    return move(far_a, 1), move(far_b, -1)


def reduce_near(high, low, got_a, got_b):
    high, low = local_call(add_far_kernel, [SLOT_ROWS] * 2, high, low, got_a, got_b)
    return move(high, 1), move(low, -1)


def finish(own, from_low, from_high):
    return local_call(add_near_kernel, [SLOT_ROWS], own, from_low, from_high)[0]


def exchange(x):
    x = x.reshape(EXP, MAIN, WIDE)
    return lax.all_to_all(x, "expert", split_axis=0, concat_axis=0, tiled=True).reshape(ROWS, WIDE)


def after(x, *others):
    return lax.optimization_barrier((x, *others))[0]


def body(tokens, expert_ids, gates, w_gate, w_up, w_down, cotangent):
    d = lax.axis_index("dp").astype(jnp.int32).reshape(1)
    swap = lambda w: lax.ppermute(w, "group", [(0, 1), (1, 0)])
    wg, wu, wd = ((hbm(w[0]), hbm(swap(w[0]))) for w in (w_gate, w_up, w_down))
    ids, gates = expert_ids.T, gates.T
    x_pack, z_pack = pack_call(d, ids, gates, tokens, cotangent)
    x_own = exchange(x_pack)
    z_own = exchange(after(z_pack, x_own))
    x_own = hbm(x_own)
    x_high, x_low = map(hbm, gather_near(x_own))
    x_far = gather_far(x_high, x_low)
    z_own = hbm(z_own)
    a, b = expert_call(
        fwd_near_kernel, d, (), (*wg, *wu), [SUMS] * 2, [IN_W] * 2, NEAR, (after(x_own, z_own), x_high, x_low)
    )
    z_high, z_low = map(hbm, gather_near(z_own))
    a, b, h, far_a, far_b = expert_call(
        fwd_far_kernel, d, (*x_far, a, b), (*wg, *wu, *wd),
        [SUMS, SUMS, UNITS, HALF_ROWS, HALF_ROWS], [IN_W, IN_W, DOWN_W], FAR,
    )
    got = reduce_far(far_a, far_b)
    out_own, out_high, out_low = expert_call(
        fwd_rest_kernel, d, (h,), wd, [SLOT_ROWS] * 3, [DOWN_W], NEAR
    )
    z_far = gather_far(z_high, z_low)
    out_low = after(out_low, z_high, z_low)
    from_low, from_high = reduce_near(out_high, out_low, *got)
    (g,) = expert_call(bwd_near_kernel, d, (), wd, [SUMS], [DOWN_W], NEAR, (z_own, z_high, z_low))
    da, db, far_a, far_b = expert_call(
        bwd_far_kernel, d, (*z_far, g, a, b), (*wg, *wu, *wd),
        [UNITS, UNITS, HALF_ROWS, HALF_ROWS], [IN_W, IN_W, DOWN_W], FAR,
    )
    got = reduce_far(far_a, far_b)
    dx_own, dx_high, dx_low = expert_call(
        bwd_rest_kernel, d, (da, db), (*wg, *wu), [SLOT_ROWS] * 3, [IN_W] * 2, NEAR
    )
    from_low = after(from_low, dx_own, *got)
    out = exchange(finish(out_own, from_low, from_high))
    from_low, from_high = reduce_near(dx_high, dx_low, *got)
    dx = exchange(finish(dx_own, from_low, from_high))
    mixed, partial = mix_call(ids, gates, cotangent, out)
    d_gates = (partial + move(partial, 2)) + (move(partial, 1) + move(partial, 3))
    d_tokens = dtok_call(ids, dx)
    return mixed, d_tokens, d_gates


def solution(mesh):
    in_specs = (
        P(("group", "expert"), None),
        P(("group", "expert"), None),
        P(("group", "expert"), None),
        P("expert", None, ("dp", "group")),
        P("expert", None, ("dp", "group")),
        P("expert", ("dp", "group"), None),
        P(("group", "expert"), "dp"),
    )
    out_specs = (
        P(("group", "expert"), "dp"),
        P(("group", "expert"), "dp"),
        P(("group", "expert"), None),
    )
    return jax.shard_map(body, mesh=mesh, in_specs=in_specs, out_specs=out_specs, check_vma=False)
```

profile of v0, /device:TPU:6, one launch (start us, length us, event | category | flops | bytes accessed | tf_op | source)
XLA Modules:
  0.0 164.0 jit_solution(4164780281054104668)
XLA Ops:
  0.6 0.1 collective-permute-start.4
  0.7 0.5 collective-permute-start.5
  1.2 0.7 copy-done.1
  1.9 0.7 copy-done.3
  2.6 3.3 %shard_map.94 = (bf16[256,1152]{1,0:T(8,128)(2,1)}, bf16[256,1152]{1,0:T(8,128)(2,1)}) custom-call(s32[1]{0:T(128)} %bitcast.2.d_ref, s32[2,128]{1,0:T(2,128)S(1)} %bitcast.16, f32[2,128]{1,0:T(2,128)S(1)} %bitcast.19, bf16[128,3584]{1,0:T(8,128)(2,1)} %tok_ref.1, bf16[128,896]{1,0:T(8,128)(2,1)} %cot_ref.3), custom_call_target="tpu_custom_call" | custom-call | flops 1000 | bytes 1000 | tf_op jit(solution)/shard_map/pallas_call | solution.py:111
  5.9 11.5 %all-to-all-start = ((bf16[32,8,1152]{2,1,0:T(8,128)(2,1)}), bf16[32,8,1152]{2,1,0:T(8,128)(2,1)S(1)}, u32[]{:S(2)}, u32[]{:S(2)}) async-start(bf16[32,8,1152]{2,1,0:T(8,128)(2,1)} %bitcast.3), calls=%async_computation | async-start | bytes 1179648 | tf_op jit(solution)/shard_map/all_to_all | solution.py:404
  17.4 0.1 collective-permute-start.6
  17.5 18.2 %all-to-all-done = bf16[32,8,1152]{2,1,0:T(8,128)(2,1)S(1)} async-done(((bf16[32,8,1152]{2,1,0:T(8,128)(2,1)}), bf16[32,8,1152]{2,1,0:T(8,128)(2,1)S(1)}, u32[]{:S(2)}, u32[]{:S(2)}) %all-to-all-start) | async-done | bytes 589856 | tf_op jit(solution)/shard_map/all_to_all | solution.py:404
  35.7 5.9 %all-to-all-start.1 = ((bf16[32,8,1152]{2,1,0:T(8,128)(2,1)}), bf16[32,8,1152]{2,1,0:T(8,128)(2,1)S(1)}, u32[]{:S(2)}, u32[]{:S(2)}) async-start(bf16[32,8,1152]{2,1,0:T(8,128)(2,1)} %bitcast.5), calls=%async_computation.1 | async-start | bytes 1179648 | tf_op jit(solution)/shard_map/all_to_all | solution.py:404
  41.5 0.9 collective-permute-start
  42.4 2.4 %collective-permute-start.1 = (bf16[256,1152]{1,0:T(8,128)(2,1)S(1)}, bf16[256,1152]{1,0:T(8,128)(2,1)S(1)}, u32[]{:S(2)}, u32[]{:S(2)}) collective-permute-start(bf16[256,1152]{1,0:T(8,128)(2,1)S(1)} %bitcast.40), channel_id=1, source_target_pairs={{0,64},{64,128},{128,192},{192,0},{1,65},{65,129},{129,193},{193,1... | collective-permute-start | bytes 1769480 | tf_op jit(solution)/shard_map/ppermute | solution.py:350
  44.9 12.5 %collective-permute-done.high = bf16[256,1152]{1,0:T(8,128)(2,1)S(1)} collective-permute-done((bf16[256,1152]{1,0:T(8,128)(2,1)S(1)}, bf16[256,1152]{1,0:T(8,128)(2,1)S(1)}, u32[]{:S(2)}, u32[]{:S(2)}) %collective-permute-start) | collective-permute-done | bytes 589856 | tf_op jit(solution)/shard_map/ppermute | solution.py:350
  57.4 0.8 copy-done.9
  58.2 0.8 copy-done.10
  59.0 1.1 shard_map.95
  60.1 2.2 %collective-permute-start.2 = (bf16[128,1152]{1,0:T(8,128)(2,1)S(1)}, bf16[128,1152]{1,0:T(8,128)(2,1)S(1)}, u32[]{:S(2)}, u32[]{:S(2)}) collective-permute-start(bf16[128,1152]{1,0:T(8,128)(2,1)S(1)} %get-tuple-element.37), channel_id=1, source_target_pairs={{0,64},{64,128},{128,192},{192,0},{1,65},{65,129},{129,193},{193,1... | collective-permute-start | bytes 884744 | tf_op jit(solution)/shard_map/ppermute | solution.py:350
  62.3 0.0 collective-permute-done.4.wg1
  62.3 0.1 collective-permute-start.7
  62.4 3.5 %collective-permute-start.8 = (bf16[256,1152]{1,0:T(8,128)(2,1)S(1)}, bf16[256,1152]{1,0:T(8,128)(2,1)S(1)}, u32[]{:S(2)}, u32[]{:S(2)}) collective-permute-start(bf16[256,1152]{1,0:T(8,128)(2,1)S(1)} %bitcast.37), channel_id=1, source_target_pairs={{0,64},{64,128},{128,192},{192,0},{1,65},{65,129},{129,193},{193,1... | collective-permute-start | bytes 1769480 | tf_op jit(solution)/shard_map/ppermute | solution.py:350
  65.9 7.5 %shard_map.96 = (f32[320,768]{1,0:T(8,128)S(1)}, f32[320,768]{1,0:T(8,128)S(1)}) custom-call(s32[1]{0:T(128)} %bitcast.2.d_ref, bf16[256,1152]{1,0:T(8,128)(2,1)} %bitcast.41, bf16[256,1152]{1,0:T(8,128)(2,1)} %copy-done.9, bf16[256,1152]{1,0:T(8,128)(2,1)} %copy-done.10, bf16[3584,384]{1,0:T(8,128)(2,1)} %bitcast.27, ...), custom_call_target="tpu_custom_call" | custom-call | flops 6000000000 | bytes 1000 | tf_op jit(solution)/shard_map/pallas_call | solution.py:272
  73.4 0.0 collective-permute-done.3.far_b
  73.5 4.6 %shard_map.97 = (f32[320,768]{1,0:T(8,128)S(1)}, f32[320,768]{1,0:T(8,128)S(1)}, bf16[320,768]{1,0:T(8,128)(2,1)S(1)}, bf16[128,1152]{1,0:T(8,128)(2,1)S(1)}, bf16[128,1152]{1,0:T(8,128)(2,1)S(1)}) custom-call(s32[1]{0:T(128)} %bitcast.2.d_ref, bf16[128,1152]{1,0:T(8,128)(2,1)S(1)} %collective-permute-done.2.far_a, ...), custom_call_target="tpu_custom_call" | custom-call | flops 1000 | bytes 1000 | tf_op jit(solution)/shard_map/pallas_call | solution.py:272
  78.1 1.8 %collective-permute-start.9 = (bf16[128,1152]{1,0:T(8,128)(2,1)S(1)}, bf16[128,1152]{1,0:T(8,128)(2,1)S(1)}, u32[]{:S(2)}, u32[]{:S(2)}) collective-permute-start(bf16[128,1152]{1,0:T(8,128)(2,1)S(1)} %get-tuple-element.49), channel_id=1, source_target_pairs={{0,64},{64,128},{128,192},{192,0},{1,65},{65,129},{129,193},{193,1... | collective-permute-start | bytes 884744 | tf_op jit(solution)/shard_map/ppermute | solution.py:350
  79.9 0.3 collective-permute-start.10
  80.2 4.0 %shard_map.98 = (bf16[256,1152]{1,0:T(8,128)(2,1)S(1)}, bf16[256,1152]{1,0:T(8,128)(2,1)S(1)}, bf16[256,1152]{1,0:T(8,128)(2,1)S(1)}) custom-call(s32[1]{0:T(128)} %bitcast.2.d_ref, bf16[320,768]{1,0:T(8,128)(2,1)S(1)} %get-tuple-element.44.h_ref, bf16[384,3584]{1,0:T(8,128)(2,1)} %bitcast.23, bf16[384,3584]{1,0:T(8,128)(2,1)} %collective-permute-done.6.wd1), custom_call_target="tpu_custom_call" | custom-call | flops 1000 | bytes 1000 | tf_op jit(solution)/shard_map/pallas_call | solution.py:272
  84.2 1.1 collective-permute-done.7.high
  85.3 0.8 copy-done.6
  86.2 0.8 copy-done.7
  87.0 1.1 shard_map.100
  88.1 1.9 %collective-permute-start.12 = (bf16[128,1152]{1,0:T(8,128)(2,1)S(1)}, bf16[128,1152]{1,0:T(8,128)(2,1)S(1)}, u32[]{:S(2)}, u32[]{:S(2)}) collective-permute-start(bf16[128,1152]{1,0:T(8,128)(2,1)S(1)} %get-tuple-element.52), channel_id=1, source_target_pairs={{0,64},{64,128},{128,192},{192,0},{1,65},{65,129},{129,193},{193,1... | collective-permute-start | bytes 884744 | tf_op jit(solution)/shard_map/ppermute | solution.py:350
  90.0 0.2 collective-permute-start.13
  90.2 0.2 shard_map.99
  90.3 3.1 %collective-permute-start.11 = (bf16[256,1152]{1,0:T(8,128)(2,1)S(1)}, bf16[256,1152]{1,0:T(8,128)(2,1)S(1)}, u32[]{:S(2)}, u32[]{:S(2)}) collective-permute-start(bf16[256,1152]{1,0:T(8,128)(2,1)S(1)} %get-tuple-element.51), channel_id=1, source_target_pairs={{0,64},{64,128},{128,192},{192,0},{1,65},{65,129},{129,193},{193,1... | collective-permute-start | bytes 1769480 | tf_op jit(solution)/shard_map/ppermute | solution.py:350
  93.5 0.0 collective-permute-start.16
  93.5 4.7 %shard_map.101.g_in = f32[320,768]{1,0:T(8,128)S(1)} custom-call(s32[1]{0:T(128)} %bitcast.2.d_ref, bf16[256,1152]{1,0:T(8,128)(2,1)} %bitcast.38, bf16[256,1152]{1,0:T(8,128)(2,1)} %copy-done.6, bf16[256,1152]{1,0:T(8,128)(2,1)} %copy-done.7, bf16[384,3584]{1,0:T(8,128)(2,1)} %bitcast.24, bf16[384,3584]{1,0:T(8,128)(2,1)} %collective-permute-done.6.wd1), custom_call_target="tpu_custom_call" | custom-call | flops 6000000000 | bytes 1000 | tf_op jit(solution)/shard_map/pallas_call | solution.py:272
  98.2 3.0 %collective-permute-done.13.far_b = bf16[128,1152]{1,0:T(8,128)(2,1)S(1)} collective-permute-done((bf16[128,1152]{1,0:T(8,128)(2,1)S(1)}, bf16[128,1152]{1,0:T(8,128)(2,1)S(1)}, u32[]{:S(2)}, u32[]{:S(2)}) %collective-permute-start.13) | collective-permute-done | bytes 294944 | tf_op jit(solution)/shard_map/ppermute | solution.py:350
  101.1 5.0 %shard_map.102 = (bf16[320,768]{1,0:T(8,128)(2,1)S(1)}, bf16[320,768]{1,0:T(8,128)(2,1)S(1)}, bf16[128,1152]{1,0:T(8,128)(2,1)S(1)}, bf16[128,1152]{1,0:T(8,128)(2,1)S(1)}) custom-call(s32[1]{0:T(128)} %bitcast.2.d_ref, bf16[128,1152]{1,0:T(8,128)(2,1)S(1)} %collective-permute-done.12.far_a, bf16[128,1152]{1,0:T(8,128)(2,1)S(1)} %collective-permute-done.13.far_b, ...), custom_call_target="tpu_custom_call" | custom-call | flops 1000 | bytes 1000 | tf_op jit(solution)/shard_map/pallas_call | solution.py:272
  106.1 0.3 collective-permute-start.14
  106.4 1.8 %collective-permute-start.15 = (bf16[128,1152]{1,0:T(8,128)(2,1)S(1)}, bf16[128,1152]{1,0:T(8,128)(2,1)S(1)}, u32[]{:S(2)}, u32[]{:S(2)}) collective-permute-start(bf16[128,1152]{1,0:T(8,128)(2,1)S(1)} %get-tuple-element.60), channel_id=1, source_target_pairs={{0,192},{64,0},{128,64},{192,128},{1,193},{65,1},{129,65},{193,129... | collective-permute-start | bytes 884744 | tf_op jit(solution)/shard_map/ppermute | solution.py:350
  108.2 6.1 %shard_map.103 = (bf16[256,1152]{1,0:T(8,128)(2,1)S(1)}, bf16[256,1152]{1,0:T(8,128)(2,1)S(1)}, bf16[256,1152]{1,0:T(8,128)(2,1)S(1)}) custom-call(s32[1]{0:T(128)} %bitcast.2.d_ref, bf16[320,768]{1,0:T(8,128)(2,1)S(1)} %get-tuple-element.56.da_ref, bf16[320,768]{1,0:T(8,128)(2,1)S(1)} %get-tuple-element.57.db_ref, bf16[3584,384]{1,0:T(8,128)(2,1)} %bitcast.30, ...), custom_call_target="tpu_custom_call" | custom-call | flops 6000000000 | bytes 1000 | tf_op jit(solution)/shard_map/pallas_call | solution.py:272
  114.3 0.9 collective-permute-done.15.got_b
  115.2 1.0 shard_map.104
  116.2 9.2 %all-to-all-start.2 = ((bf16[32,8,1152]{2,1,0:T(8,128)(2,1)}), bf16[32,8,1152]{2,1,0:T(8,128)(2,1)S(1)}, u32[]{:S(2)}, u32[]{:S(2)}) async-start(bf16[32,8,1152]{2,1,0:T(8,128)(2,1)} %bitcast.10), calls=%async_computation.2 | async-start | bytes 1179648 | tf_op jit(solution)/shard_map/all_to_all | solution.py:404
  125.5 0.0 copy-start
  125.5 0.0 copy-start.2
  125.5 0.0 copy-start.4
  125.5 0.2 shard_map.106
  125.7 1.0 collective-permute-start.17
  126.6 1.1 collective-permute-start.18
  127.8 9.5 %collective-permute-done.17.from_low = bf16[256,1152]{1,0:T(8,128)(2,1)S(1)} collective-permute-done((bf16[256,1152]{1,0:T(8,128)(2,1)S(1)}, bf16[256,1152]{1,0:T(8,128)(2,1)S(1)}, u32[]{:S(2)}, u32[]{:S(2)}) %collective-permute-start.17) | collective-permute-done | bytes 589856 | tf_op jit(solution)/shard_map/ppermute | solution.py:350
  137.3 1.3 collective-permute-done.18.from_high
  138.6 1.1 shard_map.107
  139.6 1.2 all-to-all-done.2
  140.8 8.3 %all-to-all-start.3 = ((bf16[32,8,1152]{2,1,0:T(8,128)(2,1)}), bf16[32,8,1152]{2,1,0:T(8,128)(2,1)S(1)}, u32[]{:S(2)}, u32[]{:S(2)}) async-start(bf16[32,8,1152]{2,1,0:T(8,128)(2,1)} %bitcast.12), calls=%async_computation.3 | async-start | bytes 1179648 | tf_op jit(solution)/shard_map/all_to_all | solution.py:404
  149.2 1.5 shard_map.105
  150.7 0.2 collective-permute-start.20
  150.9 1.8 %collective-permute-start.21 = (f32[128,2]{1,0:T(8,128)S(1)}, f32[128,2]{1,0:T(8,128)S(1)}, u32[]{:S(2)}, u32[]{:S(2)}) collective-permute-start(f32[128,2]{1,0:T(8,128)S(1)} %get-tuple-element.68), channel_id=1, source_target_pairs={{0,192},{64,0},{128,64},{192,128},{1,193},{65,1},{129,65},{193,129... | collective-permute-start | bytes 3080 | tf_op jit(solution)/shard_map/ppermute | solution.py:350
  152.7 0.8 collective-permute-start.19
  153.5 1.5 collective-permute-done.20
  154.9 1.4 collective-permute-done.21
  156.4 2.1 %collective-permute-done.19 = f32[128,2]{1,0:T(8,128)S(1)} collective-permute-done((f32[128,2]{1,0:T(8,128)S(1)}, f32[128,2]{1,0:T(8,128)S(1)}, u32[]{:S(2)}, u32[]{:S(2)}) %collective-permute-start.19) | collective-permute-done | bytes 1056 | tf_op jit(solution)/shard_map/ppermute | solution.py:350
  158.5 0.6 copy.10
  159.1 3.4 %all-to-all-done.3 = bf16[32,8,1152]{2,1,0:T(8,128)(2,1)S(1)} async-done(((bf16[32,8,1152]{2,1,0:T(8,128)(2,1)}), bf16[32,8,1152]{2,1,0:T(8,128)(2,1)S(1)}, u32[]{:S(2)}, u32[]{:S(2)}) %all-to-all-start.3) | async-done | bytes 589856 | tf_op jit(solution)/shard_map/all_to_all | solution.py:404
  162.6 1.4 shard_map.108
  (27 shorter events, 0.1 us)
Async XLA Ops:
  0.6 61.7 %collective-permute-start.4 = (bf16[3584,384]{1,0:T(8,128)(2,1)}, bf16[3584,384]{1,0:T(8,128)(2,1)}, u32[]{:S(2)}, u32[]{:S(2)}) collective-permute-start(bf16[3584,384]{1,0:T(8,128)(2,1)} %bitcast.26), channel_id=1, source_target_pairs={{0,32},{32,0},{1,33},{33,1},{2,34},{34,2},{3,35},{35,3},{4,36},{36... | collective-permute-start | bytes 8257544 | tf_op jit(solution)/shard_map/ppermute | solution.py:413
  0.7 61.7 %collective-permute-start.5 = (bf16[3584,384]{1,0:T(8,128)(2,1)}, bf16[3584,384]{1,0:T(8,128)(2,1)}, u32[]{:S(2)}, u32[]{:S(2)}) collective-permute-start(bf16[3584,384]{1,0:T(8,128)(2,1)} %bitcast.31), channel_id=1, source_target_pairs={{0,32},{32,0},{1,33},{33,1},{2,34},{34,2},{3,35},{35,3},{4,36},{36... | collective-permute-start | bytes 8257544 | tf_op jit(solution)/shard_map/ppermute | solution.py:413
  1.2 0.7 copy-start.1
  1.9 0.7 copy-start.3
  5.9 29.8 %all-to-all-start = ((bf16[32,8,1152]{2,1,0:T(8,128)(2,1)}), bf16[32,8,1152]{2,1,0:T(8,128)(2,1)S(1)}, u32[]{:S(2)}, u32[]{:S(2)}) async-start(bf16[32,8,1152]{2,1,0:T(8,128)(2,1)} %bitcast.3), calls=%async_computation | async-start | bytes 1179648 | tf_op jit(solution)/shard_map/all_to_all | solution.py:404
  17.4 56.1 %collective-permute-start.6 = (bf16[384,3584]{1,0:T(8,128)(2,1)}, bf16[384,3584]{1,0:T(8,128)(2,1)}, u32[]{:S(2)}, u32[]{:S(2)}) collective-permute-start(bf16[384,3584]{1,0:T(8,128)(2,1)} %bitcast.21), channel_id=1, source_target_pairs={{0,32},{32,0},{1,33},{33,1},{2,34},{34,2},{3,35},{35,3},{4,36},{36... | collective-permute-start | bytes 8257544 | tf_op jit(solution)/shard_map/ppermute | solution.py:413
  35.7 30.3 %copy-start.8 = (bf16[32,8,1152]{2,1,0:T(8,128)(2,1)}, bf16[32,8,1152]{2,1,0:T(8,128)(2,1)S(1)}, u32[]{:S(2)}) copy-start(bf16[32,8,1152]{2,1,0:T(8,128)(2,1)S(1)} %all-to-all-done) | copy-start | bytes 1769476
  35.7 26.7 %all-to-all-start.1 = ((bf16[32,8,1152]{2,1,0:T(8,128)(2,1)}), bf16[32,8,1152]{2,1,0:T(8,128)(2,1)S(1)}, u32[]{:S(2)}, u32[]{:S(2)}) async-start(bf16[32,8,1152]{2,1,0:T(8,128)(2,1)} %bitcast.5), calls=%async_computation.1 | async-start | bytes 1179648 | tf_op jit(solution)/shard_map/all_to_all | solution.py:404
  41.5 15.8 %collective-permute-start = (bf16[256,1152]{1,0:T(8,128)(2,1)S(1)}, bf16[256,1152]{1,0:T(8,128)(2,1)S(1)}, u32[]{:S(2)}, u32[]{:S(2)}) collective-permute-start(bf16[256,1152]{1,0:T(8,128)(2,1)S(1)} %bitcast.39), channel_id=1, source_target_pairs={{0,192},{64,0},{128,64},{192,128},{1,193},{65,1},{129,65},{193,129... | collective-permute-start | bytes 1769480 | tf_op jit(solution)/shard_map/ppermute | solution.py:350
  42.4 14.9 %collective-permute-start.1 = (bf16[256,1152]{1,0:T(8,128)(2,1)S(1)}, bf16[256,1152]{1,0:T(8,128)(2,1)S(1)}, u32[]{:S(2)}, u32[]{:S(2)}) collective-permute-start(bf16[256,1152]{1,0:T(8,128)(2,1)S(1)} %bitcast.40), channel_id=1, source_target_pairs={{0,64},{64,128},{128,192},{192,0},{1,65},{65,129},{129,193},{193,1... | collective-permute-start | bytes 1769480 | tf_op jit(solution)/shard_map/ppermute | solution.py:350
  57.4 0.8 copy-start.9
  58.2 0.8 copy-start.10
  60.1 13.3 %collective-permute-start.2 = (bf16[128,1152]{1,0:T(8,128)(2,1)S(1)}, bf16[128,1152]{1,0:T(8,128)(2,1)S(1)}, u32[]{:S(2)}, u32[]{:S(2)}) collective-permute-start(bf16[128,1152]{1,0:T(8,128)(2,1)S(1)} %get-tuple-element.37), channel_id=1, source_target_pairs={{0,64},{64,128},{128,192},{192,0},{1,65},{65,129},{129,193},{193,1... | collective-permute-start | bytes 884744 | tf_op jit(solution)/shard_map/ppermute | solution.py:350
  62.3 11.2 %collective-permute-start.3 = (bf16[128,1152]{1,0:T(8,128)(2,1)S(1)}, bf16[128,1152]{1,0:T(8,128)(2,1)S(1)}, u32[]{:S(2)}, u32[]{:S(2)}) collective-permute-start(bf16[128,1152]{1,0:T(8,128)(2,1)S(1)} %get-tuple-element.38), channel_id=1, source_target_pairs={{0,192},{64,0},{128,64},{192,128},{1,193},{65,1},{129,65},{193,129... | collective-permute-start | bytes 884744 | tf_op jit(solution)/shard_map/ppermute | solution.py:350
  62.3 11.1 %copy-start.5 = (bf16[32,8,1152]{2,1,0:T(8,128)(2,1)}, bf16[32,8,1152]{2,1,0:T(8,128)(2,1)S(1)}, u32[]{:S(2)}) copy-start(bf16[32,8,1152]{2,1,0:T(8,128)(2,1)S(1)} %all-to-all-done.1) | copy-start | bytes 1769476
  62.3 23.0 %collective-permute-start.7 = (bf16[256,1152]{1,0:T(8,128)(2,1)S(1)}, bf16[256,1152]{1,0:T(8,128)(2,1)S(1)}, u32[]{:S(2)}, u32[]{:S(2)}) collective-permute-start(bf16[256,1152]{1,0:T(8,128)(2,1)S(1)} %bitcast.36), channel_id=1, source_target_pairs={{0,192},{64,0},{128,64},{192,128},{1,193},{65,1},{129,65},{193,129... | collective-permute-start | bytes 1769480 | tf_op jit(solution)/shard_map/ppermute | solution.py:350
  62.4 22.9 %collective-permute-start.8 = (bf16[256,1152]{1,0:T(8,128)(2,1)S(1)}, bf16[256,1152]{1,0:T(8,128)(2,1)S(1)}, u32[]{:S(2)}, u32[]{:S(2)}) collective-permute-start(bf16[256,1152]{1,0:T(8,128)(2,1)S(1)} %bitcast.37), channel_id=1, source_target_pairs={{0,64},{64,128},{128,192},{192,0},{1,65},{65,129},{129,193},{193,1... | collective-permute-start | bytes 1769480 | tf_op jit(solution)/shard_map/ppermute | solution.py:350
  78.1 12.0 %collective-permute-start.9 = (bf16[128,1152]{1,0:T(8,128)(2,1)S(1)}, bf16[128,1152]{1,0:T(8,128)(2,1)S(1)}, u32[]{:S(2)}, u32[]{:S(2)}) collective-permute-start(bf16[128,1152]{1,0:T(8,128)(2,1)S(1)} %get-tuple-element.49), channel_id=1, source_target_pairs={{0,64},{64,128},{128,192},{192,0},{1,65},{65,129},{129,193},{193,1... | collective-permute-start | bytes 884744 | tf_op jit(solution)/shard_map/ppermute | solution.py:350
  79.9 10.3 %collective-permute-start.10 = (bf16[128,1152]{1,0:T(8,128)(2,1)S(1)}, bf16[128,1152]{1,0:T(8,128)(2,1)S(1)}, u32[]{:S(2)}, u32[]{:S(2)}) collective-permute-start(bf16[128,1152]{1,0:T(8,128)(2,1)S(1)} %get-tuple-element.50), channel_id=1, source_target_pairs={{0,192},{64,0},{128,64},{192,128},{1,193},{65,1},{129,65},{193,129... | collective-permute-start | bytes 884744 | tf_op jit(solution)/shard_map/ppermute | solution.py:350
  85.3 0.8 copy-start.6
  86.2 0.8 copy-start.7
  88.1 10.1 %collective-permute-start.12 = (bf16[128,1152]{1,0:T(8,128)(2,1)S(1)}, bf16[128,1152]{1,0:T(8,128)(2,1)S(1)}, u32[]{:S(2)}, u32[]{:S(2)}) collective-permute-start(bf16[128,1152]{1,0:T(8,128)(2,1)S(1)} %get-tuple-element.52), channel_id=1, source_target_pairs={{0,64},{64,128},{128,192},{192,0},{1,65},{65,129},{129,193},{193,1... | collective-permute-start | bytes 884744 | tf_op jit(solution)/shard_map/ppermute | solution.py:350
  90.0 11.2 %collective-permute-start.13 = (bf16[128,1152]{1,0:T(8,128)(2,1)S(1)}, bf16[128,1152]{1,0:T(8,128)(2,1)S(1)}, u32[]{:S(2)}, u32[]{:S(2)}) collective-permute-start(bf16[128,1152]{1,0:T(8,128)(2,1)S(1)} %get-tuple-element.53), channel_id=1, source_target_pairs={{0,192},{64,0},{128,64},{192,128},{1,193},{65,1},{129,65},{193,129... | collective-permute-start | bytes 884744 | tf_op jit(solution)/shard_map/ppermute | solution.py:350
  90.3 24.8 %collective-permute-start.11 = (bf16[256,1152]{1,0:T(8,128)(2,1)S(1)}, bf16[256,1152]{1,0:T(8,128)(2,1)S(1)}, u32[]{:S(2)}, u32[]{:S(2)}) collective-permute-start(bf16[256,1152]{1,0:T(8,128)(2,1)S(1)} %get-tuple-element.51), channel_id=1, source_target_pairs={{0,64},{64,128},{128,192},{192,0},{1,65},{65,129},{129,193},{193,1... | collective-permute-start | bytes 1769480 | tf_op jit(solution)/shard_map/ppermute | solution.py:350
  93.5 21.7 %collective-permute-start.16 = (bf16[256,1152]{1,0:T(8,128)(2,1)S(1)}, bf16[256,1152]{1,0:T(8,128)(2,1)S(1)}, u32[]{:S(2)}, u32[]{:S(2)}) collective-permute-start(bf16[256,1152]{1,0:T(8,128)(2,1)S(1)} %get-tuple-element.62), channel_id=1, source_target_pairs={{0,192},{64,0},{128,64},{192,128},{1,193},{65,1},{129,65},{193,129... | collective-permute-start | bytes 1769480 | tf_op jit(solution)/shard_map/ppermute | solution.py:350
  106.1 8.2 %collective-permute-start.14 = (bf16[128,1152]{1,0:T(8,128)(2,1)S(1)}, bf16[128,1152]{1,0:T(8,128)(2,1)S(1)}, u32[]{:S(2)}, u32[]{:S(2)}) collective-permute-start(bf16[128,1152]{1,0:T(8,128)(2,1)S(1)} %get-tuple-element.59), channel_id=1, source_target_pairs={{0,64},{64,128},{128,192},{192,0},{1,65},{65,129},{129,193},{193,1... | collective-permute-start | bytes 884744 | tf_op jit(solution)/shard_map/ppermute | solution.py:350
  106.4 8.8 %collective-permute-start.15 = (bf16[128,1152]{1,0:T(8,128)(2,1)S(1)}, bf16[128,1152]{1,0:T(8,128)(2,1)S(1)}, u32[]{:S(2)}, u32[]{:S(2)}) collective-permute-start(bf16[128,1152]{1,0:T(8,128)(2,1)S(1)} %get-tuple-element.60), channel_id=1, source_target_pairs={{0,192},{64,0},{128,64},{192,128},{1,193},{65,1},{129,65},{193,129... | collective-permute-start | bytes 884744 | tf_op jit(solution)/shard_map/ppermute | solution.py:350
  116.2 24.6 %all-to-all-start.2 = ((bf16[32,8,1152]{2,1,0:T(8,128)(2,1)}), bf16[32,8,1152]{2,1,0:T(8,128)(2,1)S(1)}, u32[]{:S(2)}, u32[]{:S(2)}) async-start(bf16[32,8,1152]{2,1,0:T(8,128)(2,1)} %bitcast.10), calls=%async_computation.2 | async-start | bytes 1179648 | tf_op jit(solution)/shard_map/all_to_all | solution.py:404
  125.5 23.7 %copy-start = (bf16[128,896]{1,0:T(8,128)(2,1)S(1)}, bf16[128,896]{1,0:T(8,128)(2,1)}, u32[]{:S(2)}) copy-start(bf16[128,896]{1,0:T(8,128)(2,1)} %cot_ref.3) | copy-start | bytes 688132
  125.5 23.7 %copy-start.2 = (s32[128,2]{0,1:T(2,128)S(1)}, s32[128,2]{0,1:T(2,128)}, u32[]{:S(2)}) copy-start(s32[128,2]{0,1:T(2,128)} %param.8) | copy-start | bytes 3076
  125.5 23.7 %copy-start.4 = (f32[128,2]{0,1:T(2,128)S(1)}, f32[128,2]{0,1:T(2,128)}, u32[]{:S(2)}) copy-start(f32[128,2]{0,1:T(2,128)} %param.9) | copy-start | bytes 3076
  125.7 11.6 %collective-permute-start.17 = (bf16[256,1152]{1,0:T(8,128)(2,1)S(1)}, bf16[256,1152]{1,0:T(8,128)(2,1)S(1)}, u32[]{:S(2)}, u32[]{:S(2)}) collective-permute-start(bf16[256,1152]{1,0:T(8,128)(2,1)S(1)} %get-tuple-element.66), channel_id=1, source_target_pairs={{0,64},{64,128},{128,192},{192,0},{1,65},{65,129},{129,193},{193,1... | collective-permute-start | bytes 1769480 | tf_op jit(solution)/shard_map/ppermute | solution.py:350
  126.6 11.9 %collective-permute-start.18 = (bf16[256,1152]{1,0:T(8,128)(2,1)S(1)}, bf16[256,1152]{1,0:T(8,128)(2,1)S(1)}, u32[]{:S(2)}, u32[]{:S(2)}) collective-permute-start(bf16[256,1152]{1,0:T(8,128)(2,1)S(1)} %get-tuple-element.67), channel_id=1, source_target_pairs={{0,192},{64,0},{128,64},{192,128},{1,193},{65,1},{129,65},{193,129... | collective-permute-start | bytes 1769480 | tf_op jit(solution)/shard_map/ppermute | solution.py:350
  140.8 21.8 %all-to-all-start.3 = ((bf16[32,8,1152]{2,1,0:T(8,128)(2,1)}), bf16[32,8,1152]{2,1,0:T(8,128)(2,1)S(1)}, u32[]{:S(2)}, u32[]{:S(2)}) async-start(bf16[32,8,1152]{2,1,0:T(8,128)(2,1)} %bitcast.12), calls=%async_computation.3 | async-start | bytes 1179648 | tf_op jit(solution)/shard_map/all_to_all | solution.py:404
  150.7 4.3 %collective-permute-start.20 = (f32[128,2]{1,0:T(8,128)S(1)}, f32[128,2]{1,0:T(8,128)S(1)}, u32[]{:S(2)}, u32[]{:S(2)}) collective-permute-start(f32[128,2]{1,0:T(8,128)S(1)} %get-tuple-element.68), channel_id=1, source_target_pairs={{0,64},{64,128},{128,192},{192,0},{1,65},{65,129},{129,193},{193,1... | collective-permute-start | bytes 3080 | tf_op jit(solution)/shard_map/ppermute | solution.py:350
  150.9 5.5 %collective-permute-start.21 = (f32[128,2]{1,0:T(8,128)S(1)}, f32[128,2]{1,0:T(8,128)S(1)}, u32[]{:S(2)}, u32[]{:S(2)}) collective-permute-start(f32[128,2]{1,0:T(8,128)S(1)} %get-tuple-element.68), channel_id=1, source_target_pairs={{0,192},{64,0},{128,64},{192,128},{1,193},{65,1},{129,65},{193,129... | collective-permute-start | bytes 3080 | tf_op jit(solution)/shard_map/ppermute | solution.py:350
  152.7 5.8 %collective-permute-start.19 = (f32[128,2]{1,0:T(8,128)S(1)}, f32[128,2]{1,0:T(8,128)S(1)}, u32[]{:S(2)}, u32[]{:S(2)}) collective-permute-start(f32[128,2]{1,0:T(8,128)S(1)} %get-tuple-element.68), channel_id=1, source_target_pairs={{0,128},{64,192},{128,0},{192,64},{1,129},{65,193},{129,1},{193,65... | collective-permute-start | bytes 3080 | tf_op jit(solution)/shard_map/ppermute | solution.py:350
where the time goes:
time: 166 us; the launch traced here: 164 us
  starting transfers between devices  59 us (36%)
  waiting for transfers between devices  56.1 us (34%)
  Pallas kernels  42.6 us (26%)
  local copies, waits for them, and re-layouts  5.34 us (3%)
    all_to_all x4, starting transfers between devices, exchange(): lax.all_to_all(x, 'expert', split_axis=0, concat_axis=0, tiled=True)  34.9 us
    ppermute x19, waiting for transfers between devices, move(): return lax.ppermute(x, 'dp', [(i, (i + by) % NDP) for i in range(NDP)])  33.3 us
    pallas_call x6, Pallas kernels, expert_call(): pl.pallas_call(kernel, in_specs=[pl.BlockSpec(memory_space=pltpu.SMEM)] +...  31.9 us
    ppermute x19, starting transfers between devices, move(): return lax.ppermute(x, 'dp', [(i, (i + by) % NDP) for i in range(NDP)])  23.4 us
    all_to_all x4, waiting for transfers between devices, exchange(): lax.all_to_all(x, 'expert', split_axis=0, concat_axis=0, tiled=True)  22.8 us
    unnamed x23, local copies, waits for them, and re-layouts  5.34 us
  transfers between devices with their start and end apart: 26, of which 12 were waited for; matrix products, arithmetic and copies ran while one was open for 0% of the time, Pallas kernels for 25%

commit v1 on v0

v1 whole, which is shorter than its diff:
```python
import functools
import jax
import jax.numpy as jnp
from jax import lax
from jax.experimental import pallas as pl
from jax.experimental.pallas import tpu as pltpu
from jax.sharding import PartitionSpec as P

BF = jnp.bfloat16
F32 = jnp.float32
TOK = 128
EXP = 32
MAIN = 8
OVER = 2
LANE = 128
NDP = 4
D = 3584
QD = D // NDP
CH = QD // LANE
ROWS = EXP * MAIN
WIDE = QD + OVER * LANE
ALL = ROWS + EXP * OVER
HALF = ROWS // 2
HD = 384
VMEM = 20 * 1024 * 1024
MOST = 56 * 1024 * 1024
COST = pl.CostEstimate(flops=1000, bytes_accessed=1000, transcendentals=0)
LONG_COST = pl.CostEstimate(flops=6_000_000_000, bytes_accessed=1000, transcendentals=0)
NT = (((1,), (1,)), ((), ()))
TN = (((0,), (0,)), ((), ()))


def hbm(x):
    return pltpu.with_memory_space_constraint(x, pltpu.HBM)


def params(limit=VMEM):
    return pltpu.CompilerParams(vmem_limit_bytes=limit)


def iota(shape, dim):
    return lax.broadcasted_iota(jnp.int32, shape, dim)


def dot(a, b, dims=(((1,), (0,)), ((), ()))):
    return lax.dot_general(a, b, dims, preferred_element_type=F32)


def spread(flip):
    shape = (CH * EXP, ROWS) if flip else (ROWS, CH * EXP)
    row, col = iota(shape, int(flip)), iota(shape, 1 - int(flip))
    return ((row % MAIN == col // EXP) & (row // MAIN == col % EXP)).astype(F32).astype(BF)


def pack(over):
    parts = [
        jnp.concatenate([over[c * EXP:(c + 1) * EXP, r * LANE:(r + 1) * LANE] for c in range(OVER)], axis=1)
        for r in range(CH)
    ]
    return dot(spread(False), jnp.concatenate(parts, axis=0)).astype(BF)


def unpack(packed):
    rows = dot(spread(True), packed).astype(BF)
    parts = [
        jnp.concatenate([rows[r * EXP:(r + 1) * EXP, c * LANE:(c + 1) * LANE] for c in range(OVER)], axis=0)
        for r in range(CH)
    ]
    return jnp.concatenate(parts, axis=1)


def join(piece):
    return jnp.concatenate([piece[:, :QD], unpack(piece[:, QD:])], axis=0)


def split(rows):
    return jnp.concatenate([rows[:ROWS], pack(rows[ROWS:])], axis=1)


def columns(rows):
    return [jnp.broadcast_to(rows[k:k + 1], (TOK, TOK)).T for k in range(2)]


def choose(ids):
    lane = iota((TOK, EXP), 1).astype(F32)
    cols = columns(ids.astype(F32))
    hot = [(col[:, :EXP] == lane).astype(F32) for col in cols]
    lower = (iota((TOK, TOK), 1) < iota((TOK, TOK), 0)).astype(F32).astype(BF)
    earlier = dot(lower, (hot[0] + hot[1]).astype(BF))
    out = []
    for k in range(2):
        slot = jnp.sum(earlier * hot[k], axis=1, keepdims=True)
        e = cols[k][:, :1]
        dest = jnp.where(slot < MAIN, e * MAIN + slot, ROWS + (slot - MAIN) * EXP + e).astype(jnp.int32)
        out.append((iota((TOK, ALL), 1) == dest).astype(F32).astype(BF))
    return out


def choose_rows(ids):
    lane = iota((EXP, TOK), 0)
    hot = [(lane == ids[k:k + 1]).astype(F32) for k in range(2)]
    upper = (iota((TOK, TOK), 0) < iota((TOK, TOK), 1)).astype(F32).astype(BF)
    earlier = dot((hot[0] + hot[1]).astype(BF), upper)
    out = []
    for k in range(2):
        slot = jnp.sum(earlier * hot[k], axis=0, keepdims=True).astype(jnp.int32)
        e = ids[k:k + 1]
        dest = jnp.where(slot < MAIN, e * MAIN + slot, ROWS + (slot - MAIN) * EXP + e)
        out.append((iota((ALL, TOK), 0) == dest).astype(F32))
    return out


def pack_kernel(d_ref, ids_ref, gates_ref, tok_ref, cot_ref, x_ref, z_ref):
    m0, m1 = choose_rows(ids_ref[...])
    gates = gates_ref[...]
    hot = (m0 + m1).astype(BF)
    x_ref[...] = split(dot(hot, tok_ref[...]).astype(BF))
    gate = jnp.sum(m0 * gates[0:1] + m1 * gates[1:2], axis=1, keepdims=True)
    z_ref[...] = split((gate * dot(hot, cot_ref[...])).astype(BF))


def pack_call(d, ids, gates, tokens, cot):
    full = lambda shape: pl.BlockSpec(shape, lambda i, d_ref: (0, 0))
    shape = jax.ShapeDtypeStruct((ROWS, WIDE), BF)
    return pl.pallas_call(
        pack_kernel,
        grid_spec=pltpu.PrefetchScalarGridSpec(
            num_scalar_prefetch=1,
            grid=(1,),
            in_specs=[
                full((2, TOK)),
                full((2, TOK)),
                pl.BlockSpec((TOK, QD), lambda i, d_ref: (0, d_ref[0])),
                full((TOK, QD)),
            ],
            out_specs=[full((ROWS, WIDE))] * 2,
        ),
        out_shape=[shape, shape],
        compiler_params=params(MOST),
        cost_estimate=COST,
    )(d, hbm(ids), hbm(gates), hbm(tokens), hbm(cot))


def touch_kernel(x_ref, out_ref):
    out_ref[...] = jnp.zeros_like(out_ref)


def touch_call(x):
    return pl.pallas_call(
        touch_kernel,
        in_specs=[pl.BlockSpec(memory_space=pl.ANY)],
        out_shape=jax.ShapeDtypeStruct((8, LANE), F32),
        compiler_params=params(),
        cost_estimate=LONG_COST,
    )(x)


def part_of(d, j):
    return pl.ds(pl.multiple_of(((d + j) % NDP) * QD, QD), QD)


NEAR = (0, 1, 3)
FAR = (2,)
IN_W = (QD, 2 * HD)
DOWN_W = (2 * HD, QD)


def fetch(d, pair, buf, sems, pieces, down, i):
    copies = []
    for c, w in enumerate(pair):
        own = pl.ds(c * HD, HD)
        if down:
            src, dst = w.at[:, part_of(d, pieces[i])], buf.at[i, own, :]
        else:
            src, dst = w.at[part_of(d, pieces[i]), :], buf.at[i, :, own]
        copies.append(pltpu.make_async_copy(src, dst, sems.at[i, c]))
        copies[-1].start()
    return copies


def bring(src, dst, sem):
    copy = pltpu.make_async_copy(src, dst, sem)
    copy.start()
    return copy


def wait_for(copies):
    for copy in copies:
        copy.wait()


def fetch_all(d, pair, buf, sems, pieces, down):
    return [fetch(d, pair, buf, sems, pieces, down, i) for i in range(len(pieces))]


def fwd_near_kernel(d_ref, own, high, low, wg0, wg1, wu0, wu1, sums, gate, up, gate_sem, up_sem):
    d = d_ref[0]
    weights = []
    for i in range(len(NEAR)):
        weights.append(fetch(d, (wg0, wg1), gate, gate_sem, NEAR, False, i))
        weights.append(fetch(d, (wu0, wu1), up, up_sem, NEAR, False, i))
    for i, piece in enumerate((own, high, low)):
        rows = join(piece[...])
        for k, buf in enumerate((gate, up)):
            wait_for(weights[2 * i + k])
            part = dot(rows, buf[i])
            sums[k] = part if i == 0 else sums[k] + part


def fwd_far_kernel(
    d_ref, far_a, far_b, wg0, wg1, wu0, wu1, wd0, wd1, sums,
    a_ref, b_ref, h_ref, out_a, out_b, gate, up, down, near, gate_sem, up_sem, down_sem, near_sem, in_sem,
):
    d = d_ref[0]
    gates = fetch(d, (wg0, wg1), gate, gate_sem, FAR, False, 0)
    ups = fetch(d, (wu0, wu1), up, up_sem, FAR, False, 0)
    a_copy = bring(sums.at[0], a_ref, in_sem.at[0])
    b_copy = bring(sums.at[1], b_ref, in_sem.at[1])
    downs = fetch(d, (wd0, wd1), down, down_sem, FAR, True, 0)
    nears = fetch_all(d, (wd0, wd1), near, near_sem, NEAR, True)
    rows = join(jnp.concatenate([far_a[...], far_b[...]], axis=0))
    wait_for(gates)
    part = dot(rows, gate[0])
    a_copy.wait()
    a_ref[...] = a_ref[...] + part
    wait_for(ups)
    part = dot(rows, up[0])
    b_copy.wait()
    b_ref[...] = b_ref[...] + part
    a, b = a_ref[...], b_ref[...]
    h_ref[...] = (a * jax.nn.sigmoid(a) * b).astype(BF)
    wait_for(downs)
    out = split(dot(h_ref[...], down[0]).astype(BF))
    out_a[...] = out[:HALF]
    out_b[...] = out[HALF:]
    for copies in nears:
        wait_for(copies)


def fwd_rest_kernel(d_ref, h_ref, down, wg0, wg1, own, high, low, gate, gate_sem):
    copies = fetch_all(d_ref[0], (wg0, wg1), gate, gate_sem, NEAR, False)
    for i, ref in enumerate((own, high, low)):
        ref[...] = split(dot(h_ref[...], down[i]).astype(BF))
    for copy in copies:
        wait_for(copy)


def bwd_near_kernel(d_ref, own, high, low, down, wu0, wu1, g_ref, up, up_sem):
    copies = fetch_all(d_ref[0], (wu0, wu1), up, up_sem, NEAR, False)
    for i, piece in enumerate((own, high, low)):
        part = dot(join(piece[...]), down[i], NT)
        g_ref[...] = part if i == 0 else g_ref[...] + part
    for copy in copies:
        wait_for(copy)


def bwd_far_kernel(d_ref, far_a, far_b, g_in, a_ref, b_ref, gate, up, down, da_ref, db_ref, out_a, out_b):
    rows = join(jnp.concatenate([far_a[...], far_b[...]], axis=0))
    g = g_in[...] + dot(rows, down[0], NT)
    a, b = a_ref[...], b_ref[...]
    s = jax.nn.sigmoid(a)
    da_ref[...] = (g * b * s * (1.0 + a * (1.0 - s))).astype(BF)
    db_ref[...] = (g * a * s).astype(BF)
    out = split((dot(da_ref[...], gate[0], NT) + dot(db_ref[...], up[0], NT)).astype(BF))
    out_a[...] = out[:HALF]
    out_b[...] = out[HALF:]


def bwd_rest_kernel(d_ref, da_ref, db_ref, gate, up, own, high, low):
    for i, ref in enumerate((own, high, low)):
        ref[...] = split((dot(da_ref[...], gate[i], NT) + dot(db_ref[...], up[i], NT)).astype(BF))


INSIDE = pl.BlockSpec(memory_space=pltpu.VMEM)
OUTSIDE = pl.BlockSpec(memory_space=pltpu.HBM)
HIDDEN = (ALL, 2 * HD)


def sems(*shape):
    return pltpu.SemaphoreType.DMA(shape)


def expert_call(kernel, d, inside, outside, outs, scratch=(), far_outs=()):
    return pl.pallas_call(
        kernel,
        in_specs=[pl.BlockSpec(memory_space=pltpu.SMEM)] + [INSIDE] * len(inside) + [OUTSIDE] * len(outside),
        out_specs=[INSIDE] * len(outs) + [OUTSIDE] * len(far_outs),
        out_shape=[jax.ShapeDtypeStruct(shape, kind) for shape, kind in (*outs, *far_outs)],
        scratch_shapes=list(scratch),
        compiler_params=params(),
        cost_estimate=COST if kernel in (fwd_far_kernel, fwd_rest_kernel, bwd_far_kernel) else LONG_COST,
    )(d, *inside, *outside)


def halves_kernel(high, low, low_a, high_b):
    low_a[...] = low[:HALF]
    high_b[...] = high[HALF:]


def halves_call(high, low):
    return local_call(halves_kernel, [HALF_ROWS] * 2, high, low)


SLOT_ROWS = ((ROWS, WIDE), BF)
HALF_ROWS = ((HALF, WIDE), BF)
SUMS = (HIDDEN, F32)
UNITS = (HIDDEN, BF)


def mix_kernel(ids_ref, gates_ref, cot_ref, out_ref, mixed_ref, dg_ref, hot_ref):
    hots = choose(ids_ref[...])
    hot_ref[...] = hots[0] + hots[1]
    rows = join(out_ref[...])
    gate = [col[:, :1] for col in columns(gates_ref[...])]
    cot = cot_ref[...].astype(F32)
    mixed = jnp.zeros((TOK, QD), F32)
    for k in range(2):
        mine = dot(hots[k], rows)
        mixed = mixed + gate[k] * mine
        dg_ref[:, k:k + 1] = jnp.sum(cot * mine, axis=1, keepdims=True)
    mixed_ref[...] = mixed.astype(BF)


def mix_call(ids, gates, cot, out):
    return pl.pallas_call(
        mix_kernel,
        out_shape=[
            jax.ShapeDtypeStruct((TOK, QD), BF),
            jax.ShapeDtypeStruct((TOK, 2), F32),
            jax.ShapeDtypeStruct((TOK, ALL), BF),
        ],
        compiler_params=params(),
        cost_estimate=COST,
    )(ids, gates, cot, out)


def dtok_kernel(hot_ref, dx_ref, out_ref):
    out_ref[...] = dot(hot_ref[...], join(dx_ref[...])).astype(BF)


def dtok_call(hot, dx):
    return pl.pallas_call(
        dtok_kernel,
        out_shape=jax.ShapeDtypeStruct((TOK, QD), BF),
        compiler_params=params(),
        cost_estimate=COST,
    )(hot, dx)


def move(x, by):
    return lax.ppermute(x, "dp", [(i, (i + by) % NDP) for i in range(NDP)])


def gather_near(own):
    return move(own, -1), move(own, 1)


def gather_far(high, low):
    low_a, high_b = halves_call(high, low)
    return move(low_a, 1), move(high_b, -1)


def local_call(kernel, outs, *ins):
    return pl.pallas_call(
        kernel,
        out_shape=[jax.ShapeDtypeStruct(shape, kind) for shape, kind in outs],
        compiler_params=params(),
        cost_estimate=COST,
    )(*ins)


def add(*terms):
    total = terms[0].astype(F32)
    for term in terms[1:]:
        total = total + term.astype(F32)
    return total.astype(BF)


def add_far_kernel(high, low, got_a, got_b, high_out, low_out):
    high_out[:HALF] = add(high[:HALF], got_a[...])
    high_out[HALF:] = high[HALF:]
    low_out[:HALF] = low[:HALF]
    low_out[HALF:] = add(low[HALF:], got_b[...])


def add_near_kernel(own, from_low, from_high, out):
    out[...] = add(own[...], from_low[...], from_high[...])


def reduce_far(far_a, far_b):
    return move(far_a, 1), move(far_b, -1)


def reduce_near(high, low, got_a, got_b):
    high, low = local_call(add_far_kernel, [SLOT_ROWS] * 2, high, low, got_a, got_b)
    return move(high, 1), move(low, -1)


def finish(own, from_low, from_high):
    return local_call(add_near_kernel, [SLOT_ROWS], own, from_low, from_high)[0]


def exchange(x):
    x = x.reshape(EXP, MAIN, WIDE)
    return lax.all_to_all(x, "expert", split_axis=0, concat_axis=0, tiled=True).reshape(ROWS, WIDE)


def after(x, *others):
    return lax.optimization_barrier((x, *others))[0]


def body(tokens, expert_ids, gates, w_gate, w_up, w_down, cotangent):
    d = lax.axis_index("dp").astype(jnp.int32).reshape(1)
    swap = lambda w: lax.ppermute(w, "group", [(0, 1), (1, 0)])
    wg, wu, wd = ((hbm(w[0]), hbm(swap(w[0]))) for w in (w_gate, w_up, w_down))
    ids, gates = expert_ids.T, gates.T
    x_pack, z_pack = pack_call(d, ids, gates, tokens, cotangent)
    x_own = exchange(x_pack)
    x_high, x_low = gather_near(x_own)
    z_own = exchange(after(z_pack, touch_call(x_own)))
    x_far = gather_far(x_high, x_low)
    (sums,) = expert_call(
        fwd_near_kernel, d, (x_own, x_high, x_low), (*wg, *wu), [((2, *HIDDEN), F32)],
        [pltpu.VMEM((3, *IN_W), BF)] * 2 + [sems(3, 2), sems(3, 2)],
    )
    z_own = after(z_own, sums, *x_far)
    z_high, z_low = gather_near(z_own)
    a, b, h, far_a, far_b, gate_far, up_far, down_far, down_near = expert_call(
        fwd_far_kernel, d, x_far, (*wg, *wu, *wd, hbm(sums)),
        [SUMS, SUMS, UNITS, HALF_ROWS, HALF_ROWS, *(((1, *w), BF) for w in (IN_W, IN_W, DOWN_W)), ((3, *DOWN_W), BF)],
        [sems(1, 2), sems(1, 2), sems(1, 2), sems(3, 2), sems(2)],
    )
    got = reduce_far(far_a, far_b)
    out_own, out_high, out_low, gate_near = expert_call(
        fwd_rest_kernel, d, (h, down_near), wg, [SLOT_ROWS] * 3 + [((3, *IN_W), BF)], [sems(3, 2)]
    )
    z_far = gather_far(z_high, z_low)
    g, up_near = expert_call(
        bwd_near_kernel, d, (z_own, z_high, z_low, down_near), wu, [SUMS, ((3, *IN_W), BF)], [sems(3, 2)]
    )
    out_low = after(out_low, g)
    from_low, from_high = reduce_near(out_high, out_low, *got)
    da, db, far_a, far_b = expert_call(
        bwd_far_kernel, d, (*z_far, g, a, b, gate_far, up_far, down_far), (),
        [UNITS, UNITS, HALF_ROWS, HALF_ROWS],
    )
    got = reduce_far(far_a, far_b)
    dx_own, dx_high, dx_low = expert_call(
        bwd_rest_kernel, d, (da, db, gate_near, up_near), (), [SLOT_ROWS] * 3
    )
    out = exchange(after(finish(out_own, from_low, from_high), dx_own, *got))
    from_low, from_high = reduce_near(dx_high, dx_low, *got)
    dx = exchange(finish(dx_own, from_low, from_high))
    mixed, partial, hot = mix_call(ids, gates, cotangent, out)
    d_gates = (partial + move(partial, 2)) + (move(partial, 1) + move(partial, 3))
    d_tokens = dtok_call(hot, dx)
    return mixed, d_tokens, d_gates


def solution(mesh):
    in_specs = (
        P(("group", "expert"), None),
        P(("group", "expert"), None),
        P(("group", "expert"), None),
        P("expert", None, ("dp", "group")),
        P("expert", None, ("dp", "group")),
        P("expert", ("dp", "group"), None),
        P(("group", "expert"), "dp"),
    )
    out_specs = (
        P(("group", "expert"), "dp"),
        P(("group", "expert"), "dp"),
        P(("group", "expert"), None),
    )
    return jax.shard_map(body, mesh=mesh, in_specs=in_specs, out_specs=out_specs, check_vma=False)
```

time: 166 us -> 157 us (0.946)
  Pallas kernels: 42.6 us -> 35.4 us
  local copies, waits for them, and re-layouts: 5.34 us -> 1.98 us
  starting transfers between devices: 59 us -> 62 us
    pallas_call x6, Pallas kernels: 31.9 us -> 27.3 us  [expert_call(): pl.pallas_call(kernel, in_specs=[pl.BlockSpec(memory_space=pltpu.SMEM)] +...]
    all_to_all x4, waiting for transfers between devices: 22.8 us -> 26.5 us  [exchange(): lax.all_to_all(x, 'expert', split_axis=0, concat_axis=0, tiled=True)]
    ppermute x19, waiting for transfers between devices: 33.3 us -> 29.7 us  [move(): return lax.ppermute(x, 'dp', [(i, (i + by) % NDP) for i in range(NDP)])]
    unnamed x23 -> x9, local copies, waits for them, and re-layouts: 5.34 us -> 1.98 us
    pallas_call x2 -> x0, Pallas kernels: 2.13 us -> none  [halves_call(): pl.pallas_call(halves_kernel, in_specs=[OUTSIDE] * 2, out_specs=[INSIDE]...]
    ppermute x19, starting transfers between devices: 23.4 us -> 25.1 us  [move(): return lax.ppermute(x, 'dp', [(i, (i + by) % NDP) for i in range(NDP)])]
  transfers between devices with their start and end apart: 26 -> 26, of which waited for: 12 -> 14; matrix products, arithmetic and copies ran while one was open for 0% -> 0% of each run, Pallas kernels for 25% -> 22%
where the time goes in v1:
time: 157 us; the launch traced here: 156 us
  starting transfers between devices  62 us (39%)
  waiting for transfers between devices  56.2 us (36%)
  Pallas kernels  35.4 us (23%)
  local copies, waits for them, and re-layouts  1.98 us (1%)
    all_to_all x4, starting transfers between devices, exchange(): lax.all_to_all(x, 'expert', split_axis=0, concat_axis=0, tiled=True)  36.2 us
    ppermute x19, waiting for transfers between devices, move(): return lax.ppermute(x, 'dp', [(i, (i + by) % NDP) for i in range(NDP)])  29.7 us
    pallas_call x6, Pallas kernels, expert_call(): pl.pallas_call(kernel, in_specs=[pl.BlockSpec(memory_space=pltpu.SMEM)] +...  27.3 us
    all_to_all x4, waiting for transfers between devices, exchange(): lax.all_to_all(x, 'expert', split_axis=0, concat_axis=0, tiled=True)  26.5 us
    ppermute x19, starting transfers between devices, move(): return lax.ppermute(x, 'dp', [(i, (i + by) % NDP) for i in range(NDP)])  25.1 us
  transfers between devices with their start and end apart: 26, of which 14 were waited for; matrix products, arithmetic and copies ran while one was open for 0% of the time, Pallas kernels for 22%

profile of v1, /device:TPU:6, one launch (start us, length us, event | category | flops | bytes accessed | tf_op | source)
XLA Modules:
  0.0 156.4 jit_solution(13812440178243525416)
XLA Ops:
  0.6 0.1 collective-permute-start.4
  0.7 0.5 collective-permute-start.5
  1.2 2.9 %shard_map.94 = (bf16[256,1152]{1,0:T(8,128)(2,1)}, bf16[256,1152]{1,0:T(8,128)(2,1)}) custom-call(s32[1]{0:T(128)} %bitcast.2.d_ref, s32[2,128]{1,0:T(2,128)} %bitcast.22, f32[2,128]{1,0:T(2,128)} %bitcast.24, bf16[128,3584]{1,0:T(8,128)(2,1)} %tok_ref.1, bf16[128,896]{1,0:T(8,128)(2,1)} %cot_ref.3), custom_call_target="tpu_custom_call" | custom-call | flops 1000 | bytes 1000 | tf_op jit(solution)/shard_map/pallas_call | solution.py:125
  4.1 11.5 %all-to-all-start = ((bf16[32,8,1152]{2,1,0:T(8,128)(2,1)}), bf16[32,8,1152]{2,1,0:T(8,128)(2,1)S(1)}, u32[]{:S(2)}, u32[]{:S(2)}) async-start(bf16[32,8,1152]{2,1,0:T(8,128)(2,1)} %bitcast.37), calls=%async_computation | async-start | bytes 1179648 | tf_op jit(solution)/shard_map/all_to_all | solution.py:405
  15.6 0.1 collective-permute-start.6
  15.7 18.2 %all-to-all-done = bf16[32,8,1152]{2,1,0:T(8,128)(2,1)S(1)} async-done(((bf16[32,8,1152]{2,1,0:T(8,128)(2,1)}), bf16[32,8,1152]{2,1,0:T(8,128)(2,1)S(1)}, u32[]{:S(2)}, u32[]{:S(2)}) %all-to-all-start) | async-done | bytes 589856 | tf_op jit(solution)/shard_map/all_to_all | solution.py:405
  33.9 0.8 collective-permute-start
  34.7 2.4 %collective-permute-start.1 = (bf16[256,1152]{1,0:T(8,128)(2,1)S(1)}, bf16[256,1152]{1,0:T(8,128)(2,1)S(1)}, u32[]{:S(2)}, u32[]{:S(2)}) collective-permute-start(bf16[256,1152]{1,0:T(8,128)(2,1)S(1)} %bitcast.20), channel_id=1, source_target_pairs={{0,64},{64,128},{128,192},{192,0},{1,65},{65,129},{129,193},{193,1... | collective-permute-start | bytes 1769480 | tf_op jit(solution)/shard_map/ppermute | solution.py:351
  37.1 5.9 %all-to-all-start.1 = ((bf16[32,8,1152]{2,1,0:T(8,128)(2,1)}), bf16[32,8,1152]{2,1,0:T(8,128)(2,1)S(1)}, u32[]{:S(2)}, u32[]{:S(2)}) async-start(bf16[32,8,1152]{2,1,0:T(8,128)(2,1)} %bitcast.36), calls=%async_computation.1 | async-start | bytes 1179648 | tf_op jit(solution)/shard_map/all_to_all | solution.py:405
  43.0 4.1 %collective-permute-done.high = bf16[256,1152]{1,0:T(8,128)(2,1)S(1)} collective-permute-done((bf16[256,1152]{1,0:T(8,128)(2,1)S(1)}, bf16[256,1152]{1,0:T(8,128)(2,1)S(1)}, u32[]{:S(2)}, u32[]{:S(2)}) %collective-permute-start) | collective-permute-done | bytes 589856 | tf_op jit(solution)/shard_map/ppermute | solution.py:351
  47.1 0.0 collective-permute-done.1.low
  47.2 3.4 %collective-permute-start.2 = (bf16[128,1152]{1,0:T(8,128)(2,1)S(1)}, bf16[128,1152]{1,0:T(8,128)(2,1)S(1)}, u32[]{:S(2)}, u32[]{:S(2)}) collective-permute-start(bf16[128,1152]{1,0:T(8,128)(2,1)S(1)} %get-tuple-element.42), channel_id=1, source_target_pairs={{0,64},{64,128},{128,192},{192,0},{1,65},{65,129},{129,193},{193,1... | collective-permute-start | bytes 884744 | tf_op jit(solution)/shard_map/ppermute | solution.py:351
  50.6 0.0 collective-permute-start.3
  50.6 0.0 collective-permute-done.4.wg1
  50.6 0.0 collective-permute-done.5.wu1
  50.6 6.5 %shard_map.96.sums = f32[2,320,768]{2,1,0:T(8,128)S(1)} custom-call(s32[1]{0:T(128)} %bitcast.2.d_ref, bf16[256,1152]{1,0:T(8,128)(2,1)S(1)} %bitcast.21, bf16[256,1152]{1,0:T(8,128)(2,1)S(1)} %collective-permute-done.high, bf16[256,1152]{1,0:T(8,128)(2,1)S(1)} %collective-permute-done.1.low, bf16[3584,384]{1,0:T(8,128)(2,1)} %bitcast.27, ...), custom_call_target="tpu_custom_call" | custom-call | flops 6000000000 | bytes 1000 | tf_op jit(solution)/shard_map/pallas_call | solution.py:284
  57.2 1.3 copy-done
  58.5 2.6 %all-to-all-done.1 = bf16[32,8,1152]{2,1,0:T(8,128)(2,1)S(1)} async-done(((bf16[32,8,1152]{2,1,0:T(8,128)(2,1)}), bf16[32,8,1152]{2,1,0:T(8,128)(2,1)S(1)}, u32[]{:S(2)}, u32[]{:S(2)}) %all-to-all-start.1) | async-done | bytes 589856 | tf_op jit(solution)/shard_map/all_to_all | solution.py:405
  61.1 0.0 collective-permute-done.2.far_a
  61.1 0.0 collective-permute-done.3.far_b
  61.1 0.0 collective-permute-start.7
  61.1 3.2 %collective-permute-start.8 = (bf16[256,1152]{1,0:T(8,128)(2,1)S(1)}, bf16[256,1152]{1,0:T(8,128)(2,1)S(1)}, u32[]{:S(2)}, u32[]{:S(2)}) collective-permute-start(bf16[256,1152]{1,0:T(8,128)(2,1)S(1)} %bitcast.17), channel_id=1, source_target_pairs={{0,64},{64,128},{128,192},{192,0},{1,65},{65,129},{129,193},{193,1... | collective-permute-start | bytes 1769480 | tf_op jit(solution)/shard_map/ppermute | solution.py:351
  64.3 0.0 collective-permute-done.6.wd1
  64.3 6.1 %shard_map.97 = (f32[320,768]{1,0:T(8,128)S(1)}, f32[320,768]{1,0:T(8,128)S(1)}, bf16[320,768]{1,0:T(8,128)(2,1)S(1)}, bf16[128,1152]{1,0:T(8,128)(2,1)S(1)}, bf...) custom-call(s32[1]{0:T(128)} %bitcast.2.d_ref, ...), custom_call_target="tpu_custom_call" | custom-call | flops 1000 | bytes 1000 | tf_op jit(solution)/shard_map/pallas_call | solution.py:284
  70.4 0.1 collective-permute-start.10
  70.5 3.2 %collective-permute-start.9 = (bf16[128,1152]{1,0:T(8,128)(2,1)S(1)}, bf16[128,1152]{1,0:T(8,128)(2,1)S(1)}, u32[]{:S(2)}, u32[]{:S(2)}) collective-permute-start(bf16[128,1152]{1,0:T(8,128)(2,1)S(1)} %get-tuple-element.53), channel_id=1, source_target_pairs={{0,64},{64,128},{128,192},{192,0},{1,65},{65,129},{129,193},{193,1... | collective-permute-start | bytes 884744 | tf_op jit(solution)/shard_map/ppermute | solution.py:351
  73.7 3.9 %shard_map.98 = (bf16[256,1152]{1,0:T(8,128)(2,1)S(1)}, bf16[256,1152]{1,0:T(8,128)(2,1)S(1)}, bf16[256,1152]{1,0:T(8,128)(2,1)S(1)}, bf16[3,896,768]{2,1,0:T(8,128)(2,1)S(1)}) custom-call(s32[1]{0:T(128)} %bitcast.2.d_ref, bf16[320,768]{1,0:T(8,128)(2,1)S(1)} %get-tuple-element.44.h_ref, bf16[3,768,896]{2,1,0:T(8,128)(2,1)S(1)} %get-tuple-element.45.down, ...), custom_call_target="tpu_custom_call" | custom-call | flops 1000 | bytes 1000 | tf_op jit(solution)/shard_map/pallas_call | solution.py:284
  77.6 0.0 collective-permute-done.8.low
  77.7 2.3 %collective-permute-start.13 = (bf16[128,1152]{1,0:T(8,128)(2,1)S(1)}, bf16[128,1152]{1,0:T(8,128)(2,1)S(1)}, u32[]{:S(2)}, u32[]{:S(2)}) collective-permute-start(bf16[128,1152]{1,0:T(8,128)(2,1)S(1)} %get-tuple-element.57), channel_id=1, source_target_pairs={{0,64},{64,128},{128,192},{192,0},{1,65},{65,129},{129,193},{193,1... | collective-permute-start | bytes 884744 | tf_op jit(solution)/shard_map/ppermute | solution.py:351
  80.0 0.0 collective-permute-start.14
  80.0 4.3 %shard_map.99 = (f32[320,768]{1,0:T(8,128)S(1)}, bf16[3,896,768]{2,1,0:T(8,128)(2,1)S(1)}) custom-call(s32[1]{0:T(128)} %bitcast.2.d_ref, bf16[256,1152]{1,0:T(8,128)(2,1)S(1)} %bitcast.18, bf16[256,1152]{1,0:T(8,128)(2,1)S(1)} %collective-permute-done.7.high, bf16[256,1152]{1,0:T(8,128)(2,1)S(1)} %collective-permute-done.8.low, ...), custom_call_target="tpu_custom_call" | custom-call | flops 6000000000 | bytes 1000 | tf_op jit(solution)/shard_map/pallas_call | solution.py:284
  84.3 0.2 shard_map.100
  84.5 3.3 %collective-permute-start.11 = (bf16[256,1152]{1,0:T(8,128)(2,1)S(1)}, bf16[256,1152]{1,0:T(8,128)(2,1)S(1)}, u32[]{:S(2)}, u32[]{:S(2)}) collective-permute-start(bf16[256,1152]{1,0:T(8,128)(2,1)S(1)} %get-tuple-element.55), channel_id=1, source_target_pairs={{0,64},{64,128},{128,192},{192,0},{1,65},{65,129},{129,193},{193,1... | collective-permute-start | bytes 1769480 | tf_op jit(solution)/shard_map/ppermute | solution.py:351
  87.8 0.0 collective-permute-start.12
  87.8 1.0 collective-permute-done.13.far_a
  88.8 2.3 %collective-permute-done.14.far_b = bf16[128,1152]{1,0:T(8,128)(2,1)S(1)} collective-permute-done((bf16[128,1152]{1,0:T(8,128)(2,1)S(1)}, bf16[128,1152]{1,0:T(8,128)(2,1)S(1)}, u32[]{:S(2)}, u32[]{:S(2)}) %collective-permute-start.14) | collective-permute-done | bytes 294944 | tf_op jit(solution)/shard_map/ppermute | solution.py:351
  91.1 2.8 %shard_map.103 = (bf16[320,768]{1,0:T(8,128)(2,1)S(1)}, bf16[320,768]{1,0:T(8,128)(2,1)S(1)}, bf16[128,1152]{1,0:T(8,128)(2,1)S(1)}, bf16[128,1152]{1,0:T(8,128)(2,1)S(1)}) custom-call(s32[1]{0:T(128)} %bitcast.2.d_ref, bf16[128,1152]{1,0:T(8,128)(2,1)S(1)} %collective-permute-done.13.far_a, bf16[128,1152]{1,0:T(8,128)(2,1)S(1)} %collective-permute-done.14.far_b, ...), custom_call_target="tpu_custom_call" | custom-call | flops 1000 | bytes 1000 | tf_op jit(solution)/shard_map/pallas_call | solution.py:284
  93.9 1.5 collective-permute-start.15
  95.4 0.6 collective-permute-start.16
  96.0 3.8 %shard_map.104 = (bf16[256,1152]{1,0:T(8,128)(2,1)S(1)}, bf16[256,1152]{1,0:T(8,128)(2,1)S(1)}, bf16[256,1152]{1,0:T(8,128)(2,1)S(1)}) custom-call(s32[1]{0:T(128)} %bitcast.2.d_ref, bf16[320,768]{1,0:T(8,128)(2,1)S(1)} %get-tuple-element.64.da_ref, bf16[320,768]{1,0:T(8,128)(2,1)S(1)} %get-tuple-element.65.db_ref, ...), custom_call_target="tpu_custom_call" | custom-call | flops 6000000000 | bytes 1000 | tf_op jit(solution)/shard_map/pallas_call | solution.py:284
  99.9 1.0 collective-permute-done.11.from_low
  100.9 1.5 collective-permute-done.12.from_high
  102.4 1.0 shard_map.101
  103.4 0.7 collective-permute-done.15.got_a
  104.0 1.5 collective-permute-done.16.got_b
  105.5 9.3 %all-to-all-start.2 = ((bf16[32,8,1152]{2,1,0:T(8,128)(2,1)}), bf16[32,8,1152]{2,1,0:T(8,128)(2,1)S(1)}, u32[]{:S(2)}, u32[]{:S(2)}) async-start(bf16[32,8,1152]{2,1,0:T(8,128)(2,1)} %bitcast.10), calls=%async_computation.2 | async-start | bytes 1179648 | tf_op jit(solution)/shard_map/all_to_all | solution.py:405
  114.8 0.0 copy-start.1
  114.9 0.0 copy-start.2
  114.9 0.0 copy-start.3
  114.9 0.2 shard_map.106
  115.1 1.8 %collective-permute-start.17 = (bf16[256,1152]{1,0:T(8,128)(2,1)S(1)}, bf16[256,1152]{1,0:T(8,128)(2,1)S(1)}, u32[]{:S(2)}, u32[]{:S(2)}) collective-permute-start(bf16[256,1152]{1,0:T(8,128)(2,1)S(1)} %get-tuple-element.76), channel_id=1, source_target_pairs={{0,64},{64,128},{128,192},{192,0},{1,65},{65,129},{129,193},{193,1... | collective-permute-start | bytes 1769480 | tf_op jit(solution)/shard_map/ppermute | solution.py:351
  116.9 0.3 collective-permute-start.18
  117.2 9.0 %collective-permute-done.17.from_low = bf16[256,1152]{1,0:T(8,128)(2,1)S(1)} collective-permute-done((bf16[256,1152]{1,0:T(8,128)(2,1)S(1)}, bf16[256,1152]{1,0:T(8,128)(2,1)S(1)}, u32[]{:S(2)}, u32[]{:S(2)}) %collective-permute-start.17) | collective-permute-done | bytes 589856 | tf_op jit(solution)/shard_map/ppermute | solution.py:351
  126.1 3.4 %collective-permute-done.18.from_high = bf16[256,1152]{1,0:T(8,128)(2,1)S(1)} collective-permute-done((bf16[256,1152]{1,0:T(8,128)(2,1)S(1)}, bf16[256,1152]{1,0:T(8,128)(2,1)S(1)}, u32[]{:S(2)}, u32[]{:S(2)}) %collective-permute-start.18) | collective-permute-done | bytes 589856 | tf_op jit(solution)/shard_map/ppermute | solution.py:351
  129.5 1.1 shard_map.107
  130.6 9.5 %all-to-all-start.3 = ((bf16[32,8,1152]{2,1,0:T(8,128)(2,1)}), bf16[32,8,1152]{2,1,0:T(8,128)(2,1)S(1)}, u32[]{:S(2)}, u32[]{:S(2)}) async-start(bf16[32,8,1152]{2,1,0:T(8,128)(2,1)} %bitcast.12), calls=%async_computation.3 | async-start | bytes 1179648 | tf_op jit(solution)/shard_map/all_to_all | solution.py:405
  140.1 1.5 shard_map.105
  141.7 1.7 %collective-permute-start.20 = (f32[128,2]{1,0:T(8,128)S(1)}, f32[128,2]{1,0:T(8,128)S(1)}, u32[]{:S(2)}, u32[]{:S(2)}) collective-permute-start(f32[128,2]{1,0:T(8,128)S(1)} %get-tuple-element.78), channel_id=1, source_target_pairs={{0,64},{64,128},{128,192},{192,0},{1,65},{65,129},{129,193},{193,1... | collective-permute-start | bytes 3080 | tf_op jit(solution)/shard_map/ppermute | solution.py:351
  143.4 0.3 collective-permute-start.21
  143.7 3.7 %collective-permute-done.19 = f32[128,2]{1,0:T(8,128)S(1)} collective-permute-done((f32[128,2]{1,0:T(8,128)S(1)}, f32[128,2]{1,0:T(8,128)S(1)}, u32[]{:S(2)}, u32[]{:S(2)}) %collective-permute-start.19) | collective-permute-done | bytes 1056 | tf_op jit(solution)/shard_map/ppermute | solution.py:351
  147.4 1.4 collective-permute-done.21
  148.9 0.6 copy.10
  149.6 5.8 %all-to-all-done.3 = bf16[32,8,1152]{2,1,0:T(8,128)(2,1)S(1)} async-done(((bf16[32,8,1152]{2,1,0:T(8,128)(2,1)}), bf16[32,8,1152]{2,1,0:T(8,128)(2,1)S(1)}, u32[]{:S(2)}, u32[]{:S(2)}) %all-to-all-start.3) | async-done | bytes 589856 | tf_op jit(solution)/shard_map/all_to_all | solution.py:405
  155.3 1.1 shard_map.108
  (13 shorter events, 0.1 us)
Async XLA Ops:
  0.6 50.0 %collective-permute-start.4 = (bf16[3584,384]{1,0:T(8,128)(2,1)}, bf16[3584,384]{1,0:T(8,128)(2,1)}, u32[]{:S(2)}, u32[]{:S(2)}) collective-permute-start(bf16[3584,384]{1,0:T(8,128)(2,1)} %bitcast.26), channel_id=1, source_target_pairs={{0,32},{32,0},{1,33},{33,1},{2,34},{34,2},{3,35},{35,3},{4,36},{36... | collective-permute-start | bytes 8257544 | tf_op jit(solution)/shard_map/ppermute | solution.py:414
  0.7 49.9 %collective-permute-start.5 = (bf16[3584,384]{1,0:T(8,128)(2,1)}, bf16[3584,384]{1,0:T(8,128)(2,1)}, u32[]{:S(2)}, u32[]{:S(2)}) collective-permute-start(bf16[3584,384]{1,0:T(8,128)(2,1)} %bitcast.32), channel_id=1, source_target_pairs={{0,32},{32,0},{1,33},{33,1},{2,34},{34,2},{3,35},{35,3},{4,36},{36... | collective-permute-start | bytes 8257544 | tf_op jit(solution)/shard_map/ppermute | solution.py:414
  4.1 29.8 %all-to-all-start = ((bf16[32,8,1152]{2,1,0:T(8,128)(2,1)}), bf16[32,8,1152]{2,1,0:T(8,128)(2,1)S(1)}, u32[]{:S(2)}, u32[]{:S(2)}) async-start(bf16[32,8,1152]{2,1,0:T(8,128)(2,1)} %bitcast.37), calls=%async_computation | async-start | bytes 1179648 | tf_op jit(solution)/shard_map/all_to_all | solution.py:405
  15.6 48.7 %collective-permute-start.6 = (bf16[384,3584]{1,0:T(8,128)(2,1)}, bf16[384,3584]{1,0:T(8,128)(2,1)}, u32[]{:S(2)}, u32[]{:S(2)}) collective-permute-start(bf16[384,3584]{1,0:T(8,128)(2,1)} %bitcast.30), channel_id=1, source_target_pairs={{0,32},{32,0},{1,33},{33,1},{2,34},{34,2},{3,35},{35,3},{4,36},{36... | collective-permute-start | bytes 8257544 | tf_op jit(solution)/shard_map/ppermute | solution.py:414
  33.9 13.2 %collective-permute-start = (bf16[256,1152]{1,0:T(8,128)(2,1)S(1)}, bf16[256,1152]{1,0:T(8,128)(2,1)S(1)}, u32[]{:S(2)}, u32[]{:S(2)}) collective-permute-start(bf16[256,1152]{1,0:T(8,128)(2,1)S(1)} %bitcast.19), channel_id=1, source_target_pairs={{0,192},{64,0},{128,64},{192,128},{1,193},{65,1},{129,65},{193,129... | collective-permute-start | bytes 1769480 | tf_op jit(solution)/shard_map/ppermute | solution.py:351
  34.7 12.4 %collective-permute-start.1 = (bf16[256,1152]{1,0:T(8,128)(2,1)S(1)}, bf16[256,1152]{1,0:T(8,128)(2,1)S(1)}, u32[]{:S(2)}, u32[]{:S(2)}) collective-permute-start(bf16[256,1152]{1,0:T(8,128)(2,1)S(1)} %bitcast.20), channel_id=1, source_target_pairs={{0,64},{64,128},{128,192},{192,0},{1,65},{65,129},{129,193},{193,1... | collective-permute-start | bytes 1769480 | tf_op jit(solution)/shard_map/ppermute | solution.py:351
  37.1 23.9 %all-to-all-start.1 = ((bf16[32,8,1152]{2,1,0:T(8,128)(2,1)}), bf16[32,8,1152]{2,1,0:T(8,128)(2,1)S(1)}, u32[]{:S(2)}, u32[]{:S(2)}) async-start(bf16[32,8,1152]{2,1,0:T(8,128)(2,1)} %bitcast.36), calls=%async_computation.1 | async-start | bytes 1179648 | tf_op jit(solution)/shard_map/all_to_all | solution.py:405
  47.2 13.9 %collective-permute-start.2 = (bf16[128,1152]{1,0:T(8,128)(2,1)S(1)}, bf16[128,1152]{1,0:T(8,128)(2,1)S(1)}, u32[]{:S(2)}, u32[]{:S(2)}) collective-permute-start(bf16[128,1152]{1,0:T(8,128)(2,1)S(1)} %get-tuple-element.42), channel_id=1, source_target_pairs={{0,64},{64,128},{128,192},{192,0},{1,65},{65,129},{129,193},{193,1... | collective-permute-start | bytes 884744 | tf_op jit(solution)/shard_map/ppermute | solution.py:351
  50.6 10.4 %collective-permute-start.3 = (bf16[128,1152]{1,0:T(8,128)(2,1)S(1)}, bf16[128,1152]{1,0:T(8,128)(2,1)S(1)}, u32[]{:S(2)}, u32[]{:S(2)}) collective-permute-start(bf16[128,1152]{1,0:T(8,128)(2,1)S(1)} %get-tuple-element.43), channel_id=1, source_target_pairs={{0,192},{64,0},{128,64},{192,128},{1,193},{65,1},{129,65},{193,129... | collective-permute-start | bytes 884744 | tf_op jit(solution)/shard_map/ppermute | solution.py:351
  57.2 1.3 copy-start
  61.1 16.5 %collective-permute-start.7 = (bf16[256,1152]{1,0:T(8,128)(2,1)S(1)}, bf16[256,1152]{1,0:T(8,128)(2,1)S(1)}, u32[]{:S(2)}, u32[]{:S(2)}) collective-permute-start(bf16[256,1152]{1,0:T(8,128)(2,1)S(1)} %bitcast.16), channel_id=1, source_target_pairs={{0,192},{64,0},{128,64},{192,128},{1,193},{65,1},{129,65},{193,129... | collective-permute-start | bytes 1769480 | tf_op jit(solution)/shard_map/ppermute | solution.py:351
  61.1 16.5 %collective-permute-start.8 = (bf16[256,1152]{1,0:T(8,128)(2,1)S(1)}, bf16[256,1152]{1,0:T(8,128)(2,1)S(1)}, u32[]{:S(2)}, u32[]{:S(2)}) collective-permute-start(bf16[256,1152]{1,0:T(8,128)(2,1)S(1)} %bitcast.17), channel_id=1, source_target_pairs={{0,64},{64,128},{128,192},{192,0},{1,65},{65,129},{129,193},{193,1... | collective-permute-start | bytes 1769480 | tf_op jit(solution)/shard_map/ppermute | solution.py:351
  70.4 13.9 %collective-permute-start.10 = (bf16[128,1152]{1,0:T(8,128)(2,1)S(1)}, bf16[128,1152]{1,0:T(8,128)(2,1)S(1)}, u32[]{:S(2)}, u32[]{:S(2)}) collective-permute-start(bf16[128,1152]{1,0:T(8,128)(2,1)S(1)} %get-tuple-element.54), channel_id=1, source_target_pairs={{0,192},{64,0},{128,64},{192,128},{1,193},{65,1},{129,65},{193,129... | collective-permute-start | bytes 884744 | tf_op jit(solution)/shard_map/ppermute | solution.py:351
  70.5 13.8 %collective-permute-start.9 = (bf16[128,1152]{1,0:T(8,128)(2,1)S(1)}, bf16[128,1152]{1,0:T(8,128)(2,1)S(1)}, u32[]{:S(2)}, u32[]{:S(2)}) collective-permute-start(bf16[128,1152]{1,0:T(8,128)(2,1)S(1)} %get-tuple-element.53), channel_id=1, source_target_pairs={{0,64},{64,128},{128,192},{192,0},{1,65},{65,129},{129,193},{193,1... | collective-permute-start | bytes 884744 | tf_op jit(solution)/shard_map/ppermute | solution.py:351
  77.7 11.2 %collective-permute-start.13 = (bf16[128,1152]{1,0:T(8,128)(2,1)S(1)}, bf16[128,1152]{1,0:T(8,128)(2,1)S(1)}, u32[]{:S(2)}, u32[]{:S(2)}) collective-permute-start(bf16[128,1152]{1,0:T(8,128)(2,1)S(1)} %get-tuple-element.57), channel_id=1, source_target_pairs={{0,64},{64,128},{128,192},{192,0},{1,65},{65,129},{129,193},{193,1... | collective-permute-start | bytes 884744 | tf_op jit(solution)/shard_map/ppermute | solution.py:351
  80.0 11.1 %collective-permute-start.14 = (bf16[128,1152]{1,0:T(8,128)(2,1)S(1)}, bf16[128,1152]{1,0:T(8,128)(2,1)S(1)}, u32[]{:S(2)}, u32[]{:S(2)}) collective-permute-start(bf16[128,1152]{1,0:T(8,128)(2,1)S(1)} %get-tuple-element.58), channel_id=1, source_target_pairs={{0,192},{64,0},{128,64},{192,128},{1,193},{65,1},{129,65},{193,129... | collective-permute-start | bytes 884744 | tf_op jit(solution)/shard_map/ppermute | solution.py:351
  84.5 16.4 %collective-permute-start.11 = (bf16[256,1152]{1,0:T(8,128)(2,1)S(1)}, bf16[256,1152]{1,0:T(8,128)(2,1)S(1)}, u32[]{:S(2)}, u32[]{:S(2)}) collective-permute-start(bf16[256,1152]{1,0:T(8,128)(2,1)S(1)} %get-tuple-element.55), channel_id=1, source_target_pairs={{0,64},{64,128},{128,192},{192,0},{1,65},{65,129},{129,193},{193,1... | collective-permute-start | bytes 1769480 | tf_op jit(solution)/shard_map/ppermute | solution.py:351
  87.8 14.6 %collective-permute-start.12 = (bf16[256,1152]{1,0:T(8,128)(2,1)S(1)}, bf16[256,1152]{1,0:T(8,128)(2,1)S(1)}, u32[]{:S(2)}, u32[]{:S(2)}) collective-permute-start(bf16[256,1152]{1,0:T(8,128)(2,1)S(1)} %get-tuple-element.56), channel_id=1, source_target_pairs={{0,192},{64,0},{128,64},{192,128},{1,193},{65,1},{129,65},{193,129... | collective-permute-start | bytes 1769480 | tf_op jit(solution)/shard_map/ppermute | solution.py:351
  93.9 10.1 %collective-permute-start.15 = (bf16[128,1152]{1,0:T(8,128)(2,1)S(1)}, bf16[128,1152]{1,0:T(8,128)(2,1)S(1)}, u32[]{:S(2)}, u32[]{:S(2)}) collective-permute-start(bf16[128,1152]{1,0:T(8,128)(2,1)S(1)} %get-tuple-element.69), channel_id=1, source_target_pairs={{0,64},{64,128},{128,192},{192,0},{1,65},{65,129},{129,193},{193,1... | collective-permute-start | bytes 884744 | tf_op jit(solution)/shard_map/ppermute | solution.py:351
  95.4 10.1 %collective-permute-start.16 = (bf16[128,1152]{1,0:T(8,128)(2,1)S(1)}, bf16[128,1152]{1,0:T(8,128)(2,1)S(1)}, u32[]{:S(2)}, u32[]{:S(2)}) collective-permute-start(bf16[128,1152]{1,0:T(8,128)(2,1)S(1)} %get-tuple-element.70), channel_id=1, source_target_pairs={{0,192},{64,0},{128,64},{192,128},{1,193},{65,1},{129,65},{193,129... | collective-permute-start | bytes 884744 | tf_op jit(solution)/shard_map/ppermute | solution.py:351
  105.5 25.1 %all-to-all-start.2 = ((bf16[32,8,1152]{2,1,0:T(8,128)(2,1)}), bf16[32,8,1152]{2,1,0:T(8,128)(2,1)S(1)}, u32[]{:S(2)}, u32[]{:S(2)}) async-start(bf16[32,8,1152]{2,1,0:T(8,128)(2,1)} %bitcast.10), calls=%async_computation.2 | async-start | bytes 1179648 | tf_op jit(solution)/shard_map/all_to_all | solution.py:405
  114.8 25.3 %copy-start.1 = (bf16[128,896]{1,0:T(8,128)(2,1)S(1)}, bf16[128,896]{1,0:T(8,128)(2,1)}, u32[]{:S(2)}) copy-start(bf16[128,896]{1,0:T(8,128)(2,1)} %cot_ref.3) | copy-start | bytes 688132
  114.9 25.3 %copy-start.2 = (s32[128,2]{0,1:T(2,128)S(1)}, s32[128,2]{0,1:T(2,128)}, u32[]{:S(2)}) copy-start(s32[128,2]{0,1:T(2,128)} %param.8) | copy-start | bytes 3076
  114.9 25.3 %copy-start.3 = (f32[128,2]{0,1:T(2,128)S(1)}, f32[128,2]{0,1:T(2,128)}, u32[]{:S(2)}) copy-start(f32[128,2]{0,1:T(2,128)} %param.9) | copy-start | bytes 3076
  115.1 11.1 %collective-permute-start.17 = (bf16[256,1152]{1,0:T(8,128)(2,1)S(1)}, bf16[256,1152]{1,0:T(8,128)(2,1)S(1)}, u32[]{:S(2)}, u32[]{:S(2)}) collective-permute-start(bf16[256,1152]{1,0:T(8,128)(2,1)S(1)} %get-tuple-element.76), channel_id=1, source_target_pairs={{0,64},{64,128},{128,192},{192,0},{1,65},{65,129},{129,193},{193,1... | collective-permute-start | bytes 1769480 | tf_op jit(solution)/shard_map/ppermute | solution.py:351
  116.9 12.7 %collective-permute-start.18 = (bf16[256,1152]{1,0:T(8,128)(2,1)S(1)}, bf16[256,1152]{1,0:T(8,128)(2,1)S(1)}, u32[]{:S(2)}, u32[]{:S(2)}) collective-permute-start(bf16[256,1152]{1,0:T(8,128)(2,1)S(1)} %get-tuple-element.77), channel_id=1, source_target_pairs={{0,192},{64,0},{128,64},{192,128},{1,193},{65,1},{129,65},{193,129... | collective-permute-start | bytes 1769480 | tf_op jit(solution)/shard_map/ppermute | solution.py:351
  130.6 24.7 %all-to-all-start.3 = ((bf16[32,8,1152]{2,1,0:T(8,128)(2,1)}), bf16[32,8,1152]{2,1,0:T(8,128)(2,1)S(1)}, u32[]{:S(2)}, u32[]{:S(2)}) async-start(bf16[32,8,1152]{2,1,0:T(8,128)(2,1)} %bitcast.12), calls=%async_computation.3 | async-start | bytes 1179648 | tf_op jit(solution)/shard_map/all_to_all | solution.py:405
  141.7 5.8 %collective-permute-start.19 = (f32[128,2]{1,0:T(8,128)S(1)}, f32[128,2]{1,0:T(8,128)S(1)}, u32[]{:S(2)}, u32[]{:S(2)}) collective-permute-start(f32[128,2]{1,0:T(8,128)S(1)} %get-tuple-element.78), channel_id=1, source_target_pairs={{0,128},{64,192},{128,0},{192,64},{1,129},{65,193},{129,1},{193,65... | collective-permute-start | bytes 3080 | tf_op jit(solution)/shard_map/ppermute | solution.py:351
  141.7 5.8 %collective-permute-start.20 = (f32[128,2]{1,0:T(8,128)S(1)}, f32[128,2]{1,0:T(8,128)S(1)}, u32[]{:S(2)}, u32[]{:S(2)}) collective-permute-start(f32[128,2]{1,0:T(8,128)S(1)} %get-tuple-element.78), channel_id=1, source_target_pairs={{0,64},{64,128},{128,192},{192,0},{1,65},{65,129},{129,193},{193,1... | collective-permute-start | bytes 3080 | tf_op jit(solution)/shard_map/ppermute | solution.py:351
  143.4 5.5 %collective-permute-start.21 = (f32[128,2]{1,0:T(8,128)S(1)}, f32[128,2]{1,0:T(8,128)S(1)}, u32[]{:S(2)}, u32[]{:S(2)}) collective-permute-start(f32[128,2]{1,0:T(8,128)S(1)} %get-tuple-element.78), channel_id=1, source_target_pairs={{0,192},{64,0},{128,64},{192,128},{1,193},{65,1},{129,65},{193,129... | collective-permute-start | bytes 3080 | tf_op jit(solution)/shard_map/ppermute | solution.py:351

commit v2 on v1

--- a/solution.py
+++ b/solution.py
@@ -141,7 +141,7 @@
     )(d, hbm(ids), hbm(gates), hbm(tokens), hbm(cot))
 
 
-def touch_kernel(x_ref, out_ref):
+def touch_kernel(_, out_ref):
     out_ref[...] = jnp.zeros_like(out_ref)
 
 
@@ -151,7 +151,7 @@
         in_specs=[pl.BlockSpec(memory_space=pl.ANY)],
         out_shape=jax.ShapeDtypeStruct((8, LANE), F32),
         compiler_params=params(),
-        cost_estimate=LONG_COST,
+        cost_estimate=COST,
     )(x)
 
 
@@ -208,7 +208,7 @@
 
 
 def fwd_far_kernel(
-    d_ref, far_a, far_b, wg0, wg1, wu0, wu1, wd0, wd1, sums,
+    d_ref, far_a, far_b, wg0, wg1, wu0, wu1, wd0, wd1, sums, even,
     a_ref, b_ref, h_ref, out_a, out_b, gate, up, down, near, gate_sem, up_sem, down_sem, near_sem, in_sem,
 ):
     d = d_ref[0]
@@ -417,8 +417,9 @@
     x_pack, z_pack = pack_call(d, ids, gates, tokens, cotangent)
     x_own = exchange(x_pack)
     x_high, x_low = gather_near(x_own)
-    z_own = exchange(after(z_pack, touch_call(x_own)))
+    z_own = exchange(after(z_pack, x_own))
     x_far = gather_far(x_high, x_low)
+    even = lax.ppermute(touch_call(x_low), "group", [(0, 1), (1, 0)])
     (sums,) = expert_call(
         fwd_near_kernel, d, (x_own, x_high, x_low), (*wg, *wu), [((2, *HIDDEN), F32)],
         [pltpu.VMEM((3, *IN_W), BF)] * 2 + [sems(3, 2), sems(3, 2)],
@@ -426,7 +427,7 @@
     z_own = after(z_own, sums, *x_far)
     z_high, z_low = gather_near(z_own)
     a, b, h, far_a, far_b, gate_far, up_far, down_far, down_near = expert_call(
-        fwd_far_kernel, d, x_far, (*wg, *wu, *wd, hbm(sums)),
+        fwd_far_kernel, d, x_far, (*wg, *wu, *wd, hbm(sums), even),
         [SUMS, SUMS, UNITS, HALF_ROWS, HALF_ROWS, *(((1, *w), BF) for w in (IN_W, IN_W, DOWN_W)), ((3, *DOWN_W), BF)],
         [sems(1, 2), sems(1, 2), sems(1, 2), sems(3, 2), sems(2)],
     )

time: 157 us -> 156 us (level)
  starting transfers between devices: 62 us -> 54.5 us
  waiting for transfers between devices: 56.2 us -> 62.7 us
    ppermute x19, waiting for transfers between devices: 29.7 us -> 35.5 us  [move(): return lax.ppermute(x, 'dp', [(i, (i + by) % NDP) for i in range(NDP)])]
    ppermute x19, starting transfers between devices: 25.1 us -> 20.8 us  [move(): return lax.ppermute(x, 'dp', [(i, (i + by) % NDP) for i in range(NDP)])]
    all_to_all x4, starting transfers between devices: 36.2 us -> 33 us  [exchange(): lax.all_to_all(x, 'expert', split_axis=0, concat_axis=0, tiled=True)]
  transfers between devices with their start and end apart: 26 -> 27, of which waited for: 14 -> 16; matrix products, arithmetic and copies ran while one was open for 0% -> 0% of each run, Pallas kernels for 22% -> 22%
where the time goes in v2:
time: 156 us; the launch traced here: 155 us
  waiting for transfers between devices  62.7 us (40%)
  starting transfers between devices  54.5 us (35%)
  Pallas kernels  35.4 us (23%)
  local copies, waits for them, and re-layouts  1.97 us (1%)
    ppermute x19, waiting for transfers between devices, move(): return lax.ppermute(x, 'dp', [(i, (i + by) % NDP) for i in range(NDP)])  35.5 us
    all_to_all x4, starting transfers between devices, exchange(): lax.all_to_all(x, 'expert', split_axis=0, concat_axis=0, tiled=True)  33 us
    pallas_call x6, Pallas kernels, expert_call(): pl.pallas_call(kernel, in_specs=[pl.BlockSpec(memory_space=pltpu.SMEM)] +...  27.3 us
    all_to_all x4, waiting for transfers between devices, exchange(): lax.all_to_all(x, 'expert', split_axis=0, concat_axis=0, tiled=True)  26.1 us
    ppermute x19, starting transfers between devices, move(): return lax.ppermute(x, 'dp', [(i, (i + by) % NDP) for i in range(NDP)])  20.8 us
  transfers between devices with their start and end apart: 27, of which 16 were waited for; matrix products, arithmetic and copies ran while one was open for 0% of the time, Pallas kernels for 22%

profile of v2, /device:TPU:6, one launch (start us, length us, event | category | flops | bytes accessed | tf_op | source)
XLA Modules:
  0.0 155.5 jit_solution(6553982684935814243)
XLA Ops:
  0.6 0.1 collective-permute-start.4
  0.7 0.5 collective-permute-start.5
  1.2 2.9 %shard_map.94 = (bf16[256,1152]{1,0:T(8,128)(2,1)}, bf16[256,1152]{1,0:T(8,128)(2,1)}) custom-call(s32[1]{0:T(128)} %bitcast.2.d_ref, s32[2,128]{1,0:T(2,128)} %bitcast.22, f32[2,128]{1,0:T(2,128)} %bitcast.24, bf16[128,3584]{1,0:T(8,128)(2,1)} %tok_ref.1, bf16[128,896]{1,0:T(8,128)(2,1)} %cot_ref.3), custom_call_target="tpu_custom_call" | custom-call | flops 1000 | bytes 1000 | tf_op jit(solution)/shard_map/pallas_call | solution.py:125
  4.1 11.5 %all-to-all-start = ((bf16[32,8,1152]{2,1,0:T(8,128)(2,1)}), bf16[32,8,1152]{2,1,0:T(8,128)(2,1)S(1)}, u32[]{:S(2)}, u32[]{:S(2)}) async-start(bf16[32,8,1152]{2,1,0:T(8,128)(2,1)} %bitcast.37), calls=%async_computation | async-start | bytes 1179648 | tf_op jit(solution)/shard_map/all_to_all | solution.py:405
  15.6 0.1 collective-permute-start.6
  15.7 18.2 %all-to-all-done = bf16[32,8,1152]{2,1,0:T(8,128)(2,1)S(1)} async-done(((bf16[32,8,1152]{2,1,0:T(8,128)(2,1)}), bf16[32,8,1152]{2,1,0:T(8,128)(2,1)S(1)}, u32[]{:S(2)}, u32[]{:S(2)}) %all-to-all-start) | async-done | bytes 589856 | tf_op jit(solution)/shard_map/all_to_all | solution.py:405
  33.9 0.5 collective-permute-start.1
  34.4 1.5 collective-permute-start
  35.9 5.9 %all-to-all-start.1 = ((bf16[32,8,1152]{2,1,0:T(8,128)(2,1)}), bf16[32,8,1152]{2,1,0:T(8,128)(2,1)S(1)}, u32[]{:S(2)}, u32[]{:S(2)}) async-start(bf16[32,8,1152]{2,1,0:T(8,128)(2,1)} %bitcast.36), calls=%async_computation.1 | async-start | bytes 1179648 | tf_op jit(solution)/shard_map/all_to_all | solution.py:405
  41.8 4.3 %collective-permute-done.1.low._ = bf16[256,1152]{1,0:T(8,128)(2,1)S(1)} collective-permute-done((bf16[256,1152]{1,0:T(8,128)(2,1)S(1)}, bf16[256,1152]{1,0:T(8,128)(2,1)S(1)}, u32[]{:S(2)}, u32[]{:S(2)}) %collective-permute-start.1) | collective-permute-done | bytes 589856 | tf_op jit(solution)/shard_map/ppermute | solution.py:351
  46.1 1.3 collective-permute-done.high
  47.5 0.6 collective-permute-start.2
  48.1 1.5 collective-permute-start.3
  49.6 0.0 collective-permute-done.4.wg1
  49.6 0.0 collective-permute-done.5.wu1
  49.6 6.5 %shard_map.96.sums = f32[2,320,768]{2,1,0:T(8,128)S(1)} custom-call(s32[1]{0:T(128)} %bitcast.2.d_ref, bf16[256,1152]{1,0:T(8,128)(2,1)S(1)} %bitcast.21, bf16[256,1152]{1,0:T(8,128)(2,1)S(1)} %collective-permute-done.high, bf16[256,1152]{1,0:T(8,128)(2,1)S(1)} %collective-permute-done.1.low._, bf16[3584,384]{1,0:T(8,128)(2,1)} %bitcast.27, ...), custom_call_target="tpu_custom_call" | custom-call | flops 6000000000 | bytes 1000 | tf_op jit(solution)/shard_map/pallas_call | solution.py:284
  56.2 1.3 copy-done
  57.5 0.0 collective-permute-done.3.far_b
  57.5 2.4 %all-to-all-done.1 = bf16[32,8,1152]{2,1,0:T(8,128)(2,1)S(1)} async-done(((bf16[32,8,1152]{2,1,0:T(8,128)(2,1)}), bf16[32,8,1152]{2,1,0:T(8,128)(2,1)S(1)}, u32[]{:S(2)}, u32[]{:S(2)}) %all-to-all-start.1) | async-done | bytes 589856 | tf_op jit(solution)/shard_map/all_to_all | solution.py:405
  59.8 0.8 collective-permute-start.8
  60.7 2.4 %collective-permute-start.9 = (bf16[256,1152]{1,0:T(8,128)(2,1)S(1)}, bf16[256,1152]{1,0:T(8,128)(2,1)S(1)}, u32[]{:S(2)}, u32[]{:S(2)}) collective-permute-start(bf16[256,1152]{1,0:T(8,128)(2,1)S(1)} %bitcast.17), channel_id=1, source_target_pairs={{0,64},{64,128},{128,192},{192,0},{1,65},{65,129},{129,193},{193,1... | collective-permute-start | bytes 1769480 | tf_op jit(solution)/shard_map/ppermute | solution.py:351
  63.1 0.0 collective-permute-start.7
  63.1 1.2 collective-permute-done.7.even
  64.3 0.0 collective-permute-done.6.wd1
  64.3 6.1 %shard_map.98 = (f32[320,768]{1,0:T(8,128)S(1)}, f32[320,768]{1,0:T(8,128)S(1)}, bf16[320,768]{1,0:T(8,128)(2,1)S(1)}, bf16[128,1152]{1,0:T(8,128)(2,1)S(1)}, bf...) custom-call(s32[1]{0:T(128)} %bitcast.2.d_ref, ...), custom_call_target="tpu_custom_call" | custom-call | flops 1000 | bytes 1000 | tf_op jit(solution)/shard_map/pallas_call | solution.py:284
  70.3 0.6 collective-permute-start.10
  70.9 1.5 collective-permute-start.11
  72.4 3.9 %shard_map.99 = (bf16[256,1152]{1,0:T(8,128)(2,1)S(1)}, bf16[256,1152]{1,0:T(8,128)(2,1)S(1)}, bf16[256,1152]{1,0:T(8,128)(2,1)S(1)}, bf16[3,896,768]{2,1,0:T(8,128)(2,1)S(1)}) custom-call(s32[1]{0:T(128)} %bitcast.2.d_ref, bf16[320,768]{1,0:T(8,128)(2,1)S(1)} %get-tuple-element.45.h_ref, bf16[3,768,896]{2,1,0:T(8,128)(2,1)S(1)} %get-tuple-element.46.down, ...), custom_call_target="tpu_custom_call" | custom-call | flops 1000 | bytes 1000 | tf_op jit(solution)/shard_map/pallas_call | solution.py:284
  76.4 1.8 %collective-permute-start.14 = (bf16[128,1152]{1,0:T(8,128)(2,1)S(1)}, bf16[128,1152]{1,0:T(8,128)(2,1)S(1)}, u32[]{:S(2)}, u32[]{:S(2)}) collective-permute-start(bf16[128,1152]{1,0:T(8,128)(2,1)S(1)} %get-tuple-element.59), channel_id=1, source_target_pairs={{0,64},{64,128},{128,192},{192,0},{1,65},{65,129},{129,193},{193,1... | collective-permute-start | bytes 884744 | tf_op jit(solution)/shard_map/ppermute | solution.py:351
  78.2 0.3 collective-permute-start.15
  78.5 4.3 %shard_map.100 = (f32[320,768]{1,0:T(8,128)S(1)}, bf16[3,896,768]{2,1,0:T(8,128)(2,1)S(1)}) custom-call(s32[1]{0:T(128)} %bitcast.2.d_ref, bf16[256,1152]{1,0:T(8,128)(2,1)S(1)} %bitcast.18, bf16[256,1152]{1,0:T(8,128)(2,1)S(1)} %collective-permute-done.8.high, bf16[256,1152]{1,0:T(8,128)(2,1)S(1)} %collective-permute-done.9.low, ...), custom_call_target="tpu_custom_call" | custom-call | flops 6000000000 | bytes 1000 | tf_op jit(solution)/shard_map/pallas_call | solution.py:284
  82.8 0.2 shard_map.101
  83.0 3.0 %collective-permute-start.12 = (bf16[256,1152]{1,0:T(8,128)(2,1)S(1)}, bf16[256,1152]{1,0:T(8,128)(2,1)S(1)}, u32[]{:S(2)}, u32[]{:S(2)}) collective-permute-start(bf16[256,1152]{1,0:T(8,128)(2,1)S(1)} %get-tuple-element.57), channel_id=1, source_target_pairs={{0,64},{64,128},{128,192},{192,0},{1,65},{65,129},{129,193},{193,1... | collective-permute-start | bytes 1769480 | tf_op jit(solution)/shard_map/ppermute | solution.py:351
  85.9 0.0 collective-permute-start.13
  85.9 0.6 collective-permute-done.14.far_a
  86.6 1.0 collective-permute-done.15.far_b
  87.6 2.8 %shard_map.104 = (bf16[320,768]{1,0:T(8,128)(2,1)S(1)}, bf16[320,768]{1,0:T(8,128)(2,1)S(1)}, bf16[128,1152]{1,0:T(8,128)(2,1)S(1)}, bf16[128,1152]{1,0:T(8,128)(2,1)S(1)}) custom-call(s32[1]{0:T(128)} %bitcast.2.d_ref, bf16[128,1152]{1,0:T(8,128)(2,1)S(1)} %collective-permute-done.14.far_a, bf16[128,1152]{1,0:T(8,128)(2,1)S(1)} %collective-permute-done.15.far_b, ...), custom_call_target="tpu_custom_call" | custom-call | flops 1000 | bytes 1000 | tf_op jit(solution)/shard_map/pallas_call | solution.py:284
  90.4 1.7 %collective-permute-start.16 = (bf16[128,1152]{1,0:T(8,128)(2,1)S(1)}, bf16[128,1152]{1,0:T(8,128)(2,1)S(1)}, u32[]{:S(2)}, u32[]{:S(2)}) collective-permute-start(bf16[128,1152]{1,0:T(8,128)(2,1)S(1)} %get-tuple-element.71), channel_id=1, source_target_pairs={{0,64},{64,128},{128,192},{192,0},{1,65},{65,129},{129,193},{193,1... | collective-permute-start | bytes 884744 | tf_op jit(solution)/shard_map/ppermute | solution.py:351
  92.0 0.5 collective-permute-start.17
  92.5 3.8 %shard_map.105 = (bf16[256,1152]{1,0:T(8,128)(2,1)S(1)}, bf16[256,1152]{1,0:T(8,128)(2,1)S(1)}, bf16[256,1152]{1,0:T(8,128)(2,1)S(1)}) custom-call(s32[1]{0:T(128)} %bitcast.2.d_ref, bf16[320,768]{1,0:T(8,128)(2,1)S(1)} %get-tuple-element.66.da_ref, bf16[320,768]{1,0:T(8,128)(2,1)S(1)} %get-tuple-element.67.db_ref, ...), custom_call_target="tpu_custom_call" | custom-call | flops 6000000000 | bytes 1000 | tf_op jit(solution)/shard_map/pallas_call | solution.py:284
  96.3 3.4 %collective-permute-done.12.from_low = bf16[256,1152]{1,0:T(8,128)(2,1)S(1)} collective-permute-done((bf16[256,1152]{1,0:T(8,128)(2,1)S(1)}, bf16[256,1152]{1,0:T(8,128)(2,1)S(1)}, u32[]{:S(2)}, u32[]{:S(2)}) %collective-permute-start.12) | collective-permute-done | bytes 589856 | tf_op jit(solution)/shard_map/ppermute | solution.py:351
  99.7 3.7 %collective-permute-done.13.from_high = bf16[256,1152]{1,0:T(8,128)(2,1)S(1)} collective-permute-done((bf16[256,1152]{1,0:T(8,128)(2,1)S(1)}, bf16[256,1152]{1,0:T(8,128)(2,1)S(1)}, u32[]{:S(2)}, u32[]{:S(2)}) %collective-permute-start.13) | collective-permute-done | bytes 589856 | tf_op jit(solution)/shard_map/ppermute | solution.py:351
  103.4 1.0 shard_map.102
  104.5 0.3 collective-permute-done.16.got_a
  104.8 2.7 %collective-permute-done.17.got_b = bf16[128,1152]{1,0:T(8,128)(2,1)S(1)} collective-permute-done((bf16[128,1152]{1,0:T(8,128)(2,1)S(1)}, bf16[128,1152]{1,0:T(8,128)(2,1)S(1)}, u32[]{:S(2)}, u32[]{:S(2)}) %collective-permute-start.17) | collective-permute-done | bytes 294944 | tf_op jit(solution)/shard_map/ppermute | solution.py:351
  107.5 6.1 %all-to-all-start.2 = ((bf16[32,8,1152]{2,1,0:T(8,128)(2,1)}), bf16[32,8,1152]{2,1,0:T(8,128)(2,1)S(1)}, u32[]{:S(2)}, u32[]{:S(2)}) async-start(bf16[32,8,1152]{2,1,0:T(8,128)(2,1)} %bitcast.10), calls=%async_computation.2 | async-start | bytes 1179648 | tf_op jit(solution)/shard_map/all_to_all | solution.py:405
  113.6 0.0 copy-start.1
  113.6 0.0 copy-start.2
  113.6 0.0 copy-start.3
  113.6 0.2 shard_map.107
  113.8 1.7 %collective-permute-start.18 = (bf16[256,1152]{1,0:T(8,128)(2,1)S(1)}, bf16[256,1152]{1,0:T(8,128)(2,1)S(1)}, u32[]{:S(2)}, u32[]{:S(2)}) collective-permute-start(bf16[256,1152]{1,0:T(8,128)(2,1)S(1)} %get-tuple-element.78), channel_id=1, source_target_pairs={{0,64},{64,128},{128,192},{192,0},{1,65},{65,129},{129,193},{193,1... | collective-permute-start | bytes 1769480 | tf_op jit(solution)/shard_map/ppermute | solution.py:351
  115.6 0.4 collective-permute-start.19
  115.9 9.4 %collective-permute-done.18.from_low = bf16[256,1152]{1,0:T(8,128)(2,1)S(1)} collective-permute-done((bf16[256,1152]{1,0:T(8,128)(2,1)S(1)}, bf16[256,1152]{1,0:T(8,128)(2,1)S(1)}, u32[]{:S(2)}, u32[]{:S(2)}) %collective-permute-start.18) | collective-permute-done | bytes 589856 | tf_op jit(solution)/shard_map/ppermute | solution.py:351
  125.4 3.4 %collective-permute-done.19.from_high = bf16[256,1152]{1,0:T(8,128)(2,1)S(1)} collective-permute-done((bf16[256,1152]{1,0:T(8,128)(2,1)S(1)}, bf16[256,1152]{1,0:T(8,128)(2,1)S(1)}, u32[]{:S(2)}, u32[]{:S(2)}) %collective-permute-start.19) | collective-permute-done | bytes 589856 | tf_op jit(solution)/shard_map/ppermute | solution.py:351
  128.8 1.1 shard_map.108
  129.8 9.5 %all-to-all-start.3 = ((bf16[32,8,1152]{2,1,0:T(8,128)(2,1)}), bf16[32,8,1152]{2,1,0:T(8,128)(2,1)S(1)}, u32[]{:S(2)}, u32[]{:S(2)}) async-start(bf16[32,8,1152]{2,1,0:T(8,128)(2,1)} %bitcast.12), calls=%async_computation.3 | async-start | bytes 1179648 | tf_op jit(solution)/shard_map/all_to_all | solution.py:405
  139.4 1.5 shard_map.106
  140.9 1.7 %collective-permute-start.21 = (f32[128,2]{1,0:T(8,128)S(1)}, f32[128,2]{1,0:T(8,128)S(1)}, u32[]{:S(2)}, u32[]{:S(2)}) collective-permute-start(f32[128,2]{1,0:T(8,128)S(1)} %get-tuple-element.80), channel_id=1, source_target_pairs={{0,64},{64,128},{128,192},{192,0},{1,65},{65,129},{129,193},{193,1... | collective-permute-start | bytes 3080 | tf_op jit(solution)/shard_map/ppermute | solution.py:351
  142.7 0.3 collective-permute-start.22
  142.9 3.7 %collective-permute-done.20 = f32[128,2]{1,0:T(8,128)S(1)} collective-permute-done((f32[128,2]{1,0:T(8,128)S(1)}, f32[128,2]{1,0:T(8,128)S(1)}, u32[]{:S(2)}, u32[]{:S(2)}) %collective-permute-start.20) | collective-permute-done | bytes 1056 | tf_op jit(solution)/shard_map/ppermute | solution.py:351
  146.7 1.4 collective-permute-done.22
  148.2 0.6 copy.10
  148.8 5.6 %all-to-all-done.3 = bf16[32,8,1152]{2,1,0:T(8,128)(2,1)S(1)} async-done(((bf16[32,8,1152]{2,1,0:T(8,128)(2,1)}), bf16[32,8,1152]{2,1,0:T(8,128)(2,1)S(1)}, u32[]{:S(2)}, u32[]{:S(2)}) %all-to-all-start.3) | async-done | bytes 589856 | tf_op jit(solution)/shard_map/all_to_all | solution.py:405
  154.4 1.1 shard_map.109
  (16 shorter events, 0.1 us)
Async XLA Ops:
  0.6 49.0 %collective-permute-start.4 = (bf16[3584,384]{1,0:T(8,128)(2,1)}, bf16[3584,384]{1,0:T(8,128)(2,1)}, u32[]{:S(2)}, u32[]{:S(2)}) collective-permute-start(bf16[3584,384]{1,0:T(8,128)(2,1)} %bitcast.26), channel_id=1, source_target_pairs={{0,32},{32,0},{1,33},{33,1},{2,34},{34,2},{3,35},{35,3},{4,36},{36... | collective-permute-start | bytes 8257544 | tf_op jit(solution)/shard_map/ppermute | solution.py:414
  0.7 48.9 %collective-permute-start.5 = (bf16[3584,384]{1,0:T(8,128)(2,1)}, bf16[3584,384]{1,0:T(8,128)(2,1)}, u32[]{:S(2)}, u32[]{:S(2)}) collective-permute-start(bf16[3584,384]{1,0:T(8,128)(2,1)} %bitcast.32), channel_id=1, source_target_pairs={{0,32},{32,0},{1,33},{33,1},{2,34},{34,2},{3,35},{35,3},{4,36},{36... | collective-permute-start | bytes 8257544 | tf_op jit(solution)/shard_map/ppermute | solution.py:414
  4.1 29.8 %all-to-all-start = ((bf16[32,8,1152]{2,1,0:T(8,128)(2,1)}), bf16[32,8,1152]{2,1,0:T(8,128)(2,1)S(1)}, u32[]{:S(2)}, u32[]{:S(2)}) async-start(bf16[32,8,1152]{2,1,0:T(8,128)(2,1)} %bitcast.37), calls=%async_computation | async-start | bytes 1179648 | tf_op jit(solution)/shard_map/all_to_all | solution.py:405
  15.6 48.6 %collective-permute-start.6 = (bf16[384,3584]{1,0:T(8,128)(2,1)}, bf16[384,3584]{1,0:T(8,128)(2,1)}, u32[]{:S(2)}, u32[]{:S(2)}) collective-permute-start(bf16[384,3584]{1,0:T(8,128)(2,1)} %bitcast.30), channel_id=1, source_target_pairs={{0,32},{32,0},{1,33},{33,1},{2,34},{34,2},{3,35},{35,3},{4,36},{36... | collective-permute-start | bytes 8257544 | tf_op jit(solution)/shard_map/ppermute | solution.py:414
  33.9 12.2 %collective-permute-start.1 = (bf16[256,1152]{1,0:T(8,128)(2,1)S(1)}, bf16[256,1152]{1,0:T(8,128)(2,1)S(1)}, u32[]{:S(2)}, u32[]{:S(2)}) collective-permute-start(bf16[256,1152]{1,0:T(8,128)(2,1)S(1)} %bitcast.19), channel_id=1, source_target_pairs={{0,64},{64,128},{128,192},{192,0},{1,65},{65,129},{129,193},{193,1... | collective-permute-start | bytes 1769480 | tf_op jit(solution)/shard_map/ppermute | solution.py:351
  34.4 13.1 %collective-permute-start = (bf16[256,1152]{1,0:T(8,128)(2,1)S(1)}, bf16[256,1152]{1,0:T(8,128)(2,1)S(1)}, u32[]{:S(2)}, u32[]{:S(2)}) collective-permute-start(bf16[256,1152]{1,0:T(8,128)(2,1)S(1)} %bitcast.20), channel_id=1, source_target_pairs={{0,192},{64,0},{128,64},{192,128},{1,193},{65,1},{129,65},{193,129... | collective-permute-start | bytes 1769480 | tf_op jit(solution)/shard_map/ppermute | solution.py:351
  35.9 23.9 %all-to-all-start.1 = ((bf16[32,8,1152]{2,1,0:T(8,128)(2,1)}), bf16[32,8,1152]{2,1,0:T(8,128)(2,1)S(1)}, u32[]{:S(2)}, u32[]{:S(2)}) async-start(bf16[32,8,1152]{2,1,0:T(8,128)(2,1)} %bitcast.36), calls=%async_computation.1 | async-start | bytes 1179648 | tf_op jit(solution)/shard_map/all_to_all | solution.py:405
  47.5 10.0 %collective-permute-start.2 = (bf16[128,1152]{1,0:T(8,128)(2,1)S(1)}, bf16[128,1152]{1,0:T(8,128)(2,1)S(1)}, u32[]{:S(2)}, u32[]{:S(2)}) collective-permute-start(bf16[128,1152]{1,0:T(8,128)(2,1)S(1)} %get-tuple-element.43), channel_id=1, source_target_pairs={{0,64},{64,128},{128,192},{192,0},{1,65},{65,129},{129,193},{193,1... | collective-permute-start | bytes 884744 | tf_op jit(solution)/shard_map/ppermute | solution.py:351
  48.1 9.3 %collective-permute-start.3 = (bf16[128,1152]{1,0:T(8,128)(2,1)S(1)}, bf16[128,1152]{1,0:T(8,128)(2,1)S(1)}, u32[]{:S(2)}, u32[]{:S(2)}) collective-permute-start(bf16[128,1152]{1,0:T(8,128)(2,1)S(1)} %get-tuple-element.44), channel_id=1, source_target_pairs={{0,192},{64,0},{128,64},{192,128},{1,193},{65,1},{129,65},{193,129... | collective-permute-start | bytes 884744 | tf_op jit(solution)/shard_map/ppermute | solution.py:351
  56.1 1.3 copy-start
  59.8 16.5 %collective-permute-start.8 = (bf16[256,1152]{1,0:T(8,128)(2,1)S(1)}, bf16[256,1152]{1,0:T(8,128)(2,1)S(1)}, u32[]{:S(2)}, u32[]{:S(2)}) collective-permute-start(bf16[256,1152]{1,0:T(8,128)(2,1)S(1)} %bitcast.16), channel_id=1, source_target_pairs={{0,192},{64,0},{128,64},{192,128},{1,193},{65,1},{129,65},{193,129... | collective-permute-start | bytes 1769480 | tf_op jit(solution)/shard_map/ppermute | solution.py:351
  60.7 15.7 %collective-permute-start.9 = (bf16[256,1152]{1,0:T(8,128)(2,1)S(1)}, bf16[256,1152]{1,0:T(8,128)(2,1)S(1)}, u32[]{:S(2)}, u32[]{:S(2)}) collective-permute-start(bf16[256,1152]{1,0:T(8,128)(2,1)S(1)} %bitcast.17), channel_id=1, source_target_pairs={{0,64},{64,128},{128,192},{192,0},{1,65},{65,129},{129,193},{193,1... | collective-permute-start | bytes 1769480 | tf_op jit(solution)/shard_map/ppermute | solution.py:351
  63.1 1.2 collective-permute-start.7
  70.3 12.4 %collective-permute-start.10 = (bf16[128,1152]{1,0:T(8,128)(2,1)S(1)}, bf16[128,1152]{1,0:T(8,128)(2,1)S(1)}, u32[]{:S(2)}, u32[]{:S(2)}) collective-permute-start(bf16[128,1152]{1,0:T(8,128)(2,1)S(1)} %get-tuple-element.55), channel_id=1, source_target_pairs={{0,64},{64,128},{128,192},{192,0},{1,65},{65,129},{129,193},{193,1... | collective-permute-start | bytes 884744 | tf_op jit(solution)/shard_map/ppermute | solution.py:351
  70.9 11.9 %collective-permute-start.11 = (bf16[128,1152]{1,0:T(8,128)(2,1)S(1)}, bf16[128,1152]{1,0:T(8,128)(2,1)S(1)}, u32[]{:S(2)}, u32[]{:S(2)}) collective-permute-start(bf16[128,1152]{1,0:T(8,128)(2,1)S(1)} %get-tuple-element.56), channel_id=1, source_target_pairs={{0,192},{64,0},{128,64},{192,128},{1,193},{65,1},{129,65},{193,129... | collective-permute-start | bytes 884744 | tf_op jit(solution)/shard_map/ppermute | solution.py:351
  76.4 10.2 %collective-permute-start.14 = (bf16[128,1152]{1,0:T(8,128)(2,1)S(1)}, bf16[128,1152]{1,0:T(8,128)(2,1)S(1)}, u32[]{:S(2)}, u32[]{:S(2)}) collective-permute-start(bf16[128,1152]{1,0:T(8,128)(2,1)S(1)} %get-tuple-element.59), channel_id=1, source_target_pairs={{0,64},{64,128},{128,192},{192,0},{1,65},{65,129},{129,193},{193,1... | collective-permute-start | bytes 884744 | tf_op jit(solution)/shard_map/ppermute | solution.py:351
  78.2 9.5 %collective-permute-start.15 = (bf16[128,1152]{1,0:T(8,128)(2,1)S(1)}, bf16[128,1152]{1,0:T(8,128)(2,1)S(1)}, u32[]{:S(2)}, u32[]{:S(2)}) collective-permute-start(bf16[128,1152]{1,0:T(8,128)(2,1)S(1)} %get-tuple-element.60), channel_id=1, source_target_pairs={{0,192},{64,0},{128,64},{192,128},{1,193},{65,1},{129,65},{193,129... | collective-permute-start | bytes 884744 | tf_op jit(solution)/shard_map/ppermute | solution.py:351
  83.0 16.8 %collective-permute-start.12 = (bf16[256,1152]{1,0:T(8,128)(2,1)S(1)}, bf16[256,1152]{1,0:T(8,128)(2,1)S(1)}, u32[]{:S(2)}, u32[]{:S(2)}) collective-permute-start(bf16[256,1152]{1,0:T(8,128)(2,1)S(1)} %get-tuple-element.57), channel_id=1, source_target_pairs={{0,64},{64,128},{128,192},{192,0},{1,65},{65,129},{129,193},{193,1... | collective-permute-start | bytes 1769480 | tf_op jit(solution)/shard_map/ppermute | solution.py:351
  85.9 17.5 %collective-permute-start.13 = (bf16[256,1152]{1,0:T(8,128)(2,1)S(1)}, bf16[256,1152]{1,0:T(8,128)(2,1)S(1)}, u32[]{:S(2)}, u32[]{:S(2)}) collective-permute-start(bf16[256,1152]{1,0:T(8,128)(2,1)S(1)} %get-tuple-element.58), channel_id=1, source_target_pairs={{0,192},{64,0},{128,64},{192,128},{1,193},{65,1},{129,65},{193,129... | collective-permute-start | bytes 1769480 | tf_op jit(solution)/shard_map/ppermute | solution.py:351
  90.4 14.4 %collective-permute-start.16 = (bf16[128,1152]{1,0:T(8,128)(2,1)S(1)}, bf16[128,1152]{1,0:T(8,128)(2,1)S(1)}, u32[]{:S(2)}, u32[]{:S(2)}) collective-permute-start(bf16[128,1152]{1,0:T(8,128)(2,1)S(1)} %get-tuple-element.71), channel_id=1, source_target_pairs={{0,64},{64,128},{128,192},{192,0},{1,65},{65,129},{129,193},{193,1... | collective-permute-start | bytes 884744 | tf_op jit(solution)/shard_map/ppermute | solution.py:351
  92.0 15.4 %collective-permute-start.17 = (bf16[128,1152]{1,0:T(8,128)(2,1)S(1)}, bf16[128,1152]{1,0:T(8,128)(2,1)S(1)}, u32[]{:S(2)}, u32[]{:S(2)}) collective-permute-start(bf16[128,1152]{1,0:T(8,128)(2,1)S(1)} %get-tuple-element.72), channel_id=1, source_target_pairs={{0,192},{64,0},{128,64},{192,128},{1,193},{65,1},{129,65},{193,129... | collective-permute-start | bytes 884744 | tf_op jit(solution)/shard_map/ppermute | solution.py:351
  107.5 22.4 %all-to-all-start.2 = ((bf16[32,8,1152]{2,1,0:T(8,128)(2,1)}), bf16[32,8,1152]{2,1,0:T(8,128)(2,1)S(1)}, u32[]{:S(2)}, u32[]{:S(2)}) async-start(bf16[32,8,1152]{2,1,0:T(8,128)(2,1)} %bitcast.10), calls=%async_computation.2 | async-start | bytes 1179648 | tf_op jit(solution)/shard_map/all_to_all | solution.py:405
  113.6 25.7 %copy-start.1 = (bf16[128,896]{1,0:T(8,128)(2,1)S(1)}, bf16[128,896]{1,0:T(8,128)(2,1)}, u32[]{:S(2)}) copy-start(bf16[128,896]{1,0:T(8,128)(2,1)} %cot_ref.3) | copy-start | bytes 688132
  113.6 25.7 %copy-start.2 = (s32[128,2]{0,1:T(2,128)S(1)}, s32[128,2]{0,1:T(2,128)}, u32[]{:S(2)}) copy-start(s32[128,2]{0,1:T(2,128)} %param.8) | copy-start | bytes 3076
  113.6 25.7 %copy-start.3 = (f32[128,2]{0,1:T(2,128)S(1)}, f32[128,2]{0,1:T(2,128)}, u32[]{:S(2)}) copy-start(f32[128,2]{0,1:T(2,128)} %param.9) | copy-start | bytes 3076
  113.8 11.5 %collective-permute-start.18 = (bf16[256,1152]{1,0:T(8,128)(2,1)S(1)}, bf16[256,1152]{1,0:T(8,128)(2,1)S(1)}, u32[]{:S(2)}, u32[]{:S(2)}) collective-permute-start(bf16[256,1152]{1,0:T(8,128)(2,1)S(1)} %get-tuple-element.78), channel_id=1, source_target_pairs={{0,64},{64,128},{128,192},{192,0},{1,65},{65,129},{129,193},{193,1... | collective-permute-start | bytes 1769480 | tf_op jit(solution)/shard_map/ppermute | solution.py:351
  115.6 13.2 %collective-permute-start.19 = (bf16[256,1152]{1,0:T(8,128)(2,1)S(1)}, bf16[256,1152]{1,0:T(8,128)(2,1)S(1)}, u32[]{:S(2)}, u32[]{:S(2)}) collective-permute-start(bf16[256,1152]{1,0:T(8,128)(2,1)S(1)} %get-tuple-element.79), channel_id=1, source_target_pairs={{0,192},{64,0},{128,64},{192,128},{1,193},{65,1},{129,65},{193,129... | collective-permute-start | bytes 1769480 | tf_op jit(solution)/shard_map/ppermute | solution.py:351
  129.8 24.5 %all-to-all-start.3 = ((bf16[32,8,1152]{2,1,0:T(8,128)(2,1)}), bf16[32,8,1152]{2,1,0:T(8,128)(2,1)S(1)}, u32[]{:S(2)}, u32[]{:S(2)}) async-start(bf16[32,8,1152]{2,1,0:T(8,128)(2,1)} %bitcast.12), calls=%async_computation.3 | async-start | bytes 1179648 | tf_op jit(solution)/shard_map/all_to_all | solution.py:405
  140.9 5.8 %collective-permute-start.20 = (f32[128,2]{1,0:T(8,128)S(1)}, f32[128,2]{1,0:T(8,128)S(1)}, u32[]{:S(2)}, u32[]{:S(2)}) collective-permute-start(f32[128,2]{1,0:T(8,128)S(1)} %get-tuple-element.80), channel_id=1, source_target_pairs={{0,128},{64,192},{128,0},{192,64},{1,129},{65,193},{129,1},{193,65... | collective-permute-start | bytes 3080 | tf_op jit(solution)/shard_map/ppermute | solution.py:351
  140.9 5.8 %collective-permute-start.21 = (f32[128,2]{1,0:T(8,128)S(1)}, f32[128,2]{1,0:T(8,128)S(1)}, u32[]{:S(2)}, u32[]{:S(2)}) collective-permute-start(f32[128,2]{1,0:T(8,128)S(1)} %get-tuple-element.80), channel_id=1, source_target_pairs={{0,64},{64,128},{128,192},{192,0},{1,65},{65,129},{129,193},{193,1... | collective-permute-start | bytes 3080 | tf_op jit(solution)/shard_map/ppermute | solution.py:351
  142.7 5.5 %collective-permute-start.22 = (f32[128,2]{1,0:T(8,128)S(1)}, f32[128,2]{1,0:T(8,128)S(1)}, u32[]{:S(2)}, u32[]{:S(2)}) collective-permute-start(f32[128,2]{1,0:T(8,128)S(1)} %get-tuple-element.80), channel_id=1, source_target_pairs={{0,192},{64,0},{128,64},{192,128},{1,193},{65,1},{129,65},{193,129... | collective-permute-start | bytes 3080 | tf_op jit(solution)/shard_map/ppermute | solution.py:351

commit v3 on v2

--- a/solution.py
+++ b/solution.py
@@ -208,7 +208,7 @@
 
 
 def fwd_far_kernel(
-    d_ref, far_a, far_b, wg0, wg1, wu0, wu1, wd0, wd1, sums, even,
+    d_ref, far_a, far_b, wg0, wg1, wu0, wu1, wd0, wd1, sums,
     a_ref, b_ref, h_ref, out_a, out_b, gate, up, down, near, gate_sem, up_sem, down_sem, near_sem, in_sem,
 ):
     d = d_ref[0]
@@ -217,13 +217,13 @@
     a_copy = bring(sums.at[0], a_ref, in_sem.at[0])
     b_copy = bring(sums.at[1], b_ref, in_sem.at[1])
     downs = fetch(d, (wd0, wd1), down, down_sem, FAR, True, 0)
-    nears = fetch_all(d, (wd0, wd1), near, near_sem, NEAR, True)
     rows = join(jnp.concatenate([far_a[...], far_b[...]], axis=0))
     wait_for(gates)
     part = dot(rows, gate[0])
     a_copy.wait()
     a_ref[...] = a_ref[...] + part
     wait_for(ups)
+    nears = fetch_all(d, (wd0, wd1), near, near_sem, NEAR, True)
     part = dot(rows, up[0])
     b_copy.wait()
     b_ref[...] = b_ref[...] + part
@@ -237,7 +237,7 @@
         wait_for(copies)
 
 
-def fwd_rest_kernel(d_ref, h_ref, down, wg0, wg1, own, high, low, gate, gate_sem):
+def fwd_rest_kernel(d_ref, h_ref, down, wg0, wg1, _, own, high, low, gate, gate_sem):
     copies = fetch_all(d_ref[0], (wg0, wg1), gate, gate_sem, NEAR, False)
     for i, ref in enumerate((own, high, low)):
         ref[...] = split(dot(h_ref[...], down[i]).astype(BF))
@@ -288,7 +288,7 @@
         out_shape=[jax.ShapeDtypeStruct(shape, kind) for shape, kind in (*outs, *far_outs)],
         scratch_shapes=list(scratch),
         compiler_params=params(),
-        cost_estimate=COST if kernel in (fwd_far_kernel, fwd_rest_kernel, bwd_far_kernel) else LONG_COST,
+        cost_estimate=COST if kernel in (fwd_rest_kernel, bwd_far_kernel) else LONG_COST,
     )(d, *inside, *outside)
 
 
@@ -427,13 +427,13 @@
     z_own = after(z_own, sums, *x_far)
     z_high, z_low = gather_near(z_own)
     a, b, h, far_a, far_b, gate_far, up_far, down_far, down_near = expert_call(
-        fwd_far_kernel, d, x_far, (*wg, *wu, *wd, hbm(sums), even),
+        fwd_far_kernel, d, x_far, (*wg, *wu, *wd, hbm(sums)),
         [SUMS, SUMS, UNITS, HALF_ROWS, HALF_ROWS, *(((1, *w), BF) for w in (IN_W, IN_W, DOWN_W)), ((3, *DOWN_W), BF)],
         [sems(1, 2), sems(1, 2), sems(1, 2), sems(3, 2), sems(2)],
     )
     got = reduce_far(far_a, far_b)
     out_own, out_high, out_low, gate_near = expert_call(
-        fwd_rest_kernel, d, (h, down_near), wg, [SLOT_ROWS] * 3 + [((3, *IN_W), BF)], [sems(3, 2)]
+        fwd_rest_kernel, d, (h, down_near), (*wg, even), [SLOT_ROWS] * 3 + [((3, *IN_W), BF)], [sems(3, 2)]
     )
     z_far = gather_far(z_high, z_low)
     g, up_near = expert_call(

time: 156 us -> 156 us (level)
  blocking collectives: 0 us -> 30.1 us
  waiting for transfers between devices: 62.7 us -> 43.5 us
  starting transfers between devices: 54.5 us -> 44.7 us
    all_to_all x0 -> x1, blocking collectives: none -> 30.1 us  [exchange(): lax.all_to_all(x, 'expert', split_axis=0, concat_axis=0, tiled=True)]
    all_to_all x4 -> x3, waiting for transfers between devices: 26.1 us -> 7.72 us  [exchange(): lax.all_to_all(x, 'expert', split_axis=0, concat_axis=0, tiled=True)]
    all_to_all x4 -> x3, starting transfers between devices: 33 us -> 23.2 us  [exchange(): lax.all_to_all(x, 'expert', split_axis=0, concat_axis=0, tiled=True)]
  transfers between devices with their start and end apart: 27 -> 26, of which waited for: 16 -> 14; matrix products, arithmetic and copies ran while one was open for 0% -> 0% of each run, Pallas kernels for 22% -> 22%
where the time goes in v3:
time: 156 us
  starting transfers between devices  44.7 us (29%)
  waiting for transfers between devices  43.5 us (28%)
  Pallas kernels  34.8 us (22%)
  blocking collectives  30.1 us (19%)
  local copies, waits for them, and re-layouts  1.98 us (1%)
    ppermute x19, waiting for transfers between devices, move(): return lax.ppermute(x, 'dp', [(i, (i + by) % NDP) for i in range(NDP)])  35.7 us
    all_to_all x1, blocking collectives, exchange(): lax.all_to_all(x, 'expert', split_axis=0, concat_axis=0, tiled=True)  30.1 us
    pallas_call x6, Pallas kernels, expert_call(): pl.pallas_call(kernel, in_specs=[pl.BlockSpec(memory_space=pltpu.SMEM)] +...  26.7 us
    all_to_all x3, starting transfers between devices, exchange(): lax.all_to_all(x, 'expert', split_axis=0, concat_axis=0, tiled=True)  23.2 us
    ppermute x19, starting transfers between devices, move(): return lax.ppermute(x, 'dp', [(i, (i + by) % NDP) for i in range(NDP)])  20.8 us
    all_to_all x3, waiting for transfers between devices, exchange(): lax.all_to_all(x, 'expert', split_axis=0, concat_axis=0, tiled=True)  7.72 us
  transfers between devices with their start and end apart: 26, of which 14 were waited for; matrix products, arithmetic and copies ran while one was open for 0% of the time, Pallas kernels for 22%

profile of v3, /device:TPU:6, one launch (start us, length us, event | category | flops | bytes accessed | tf_op | source)
XLA Modules:
  0.0 155.8 jit_solution(14473792985859739530)
XLA Ops:
  0.6 0.1 collective-permute-start.4
  0.7 0.5 collective-permute-start.5
  1.2 0.1 collective-permute-start.6
  1.3 2.9 %shard_map.94 = (bf16[256,1152]{1,0:T(8,128)(2,1)}, bf16[256,1152]{1,0:T(8,128)(2,1)}) custom-call(s32[1]{0:T(128)} %bitcast.2.d_ref, s32[2,128]{1,0:T(2,128)} %bitcast.22, f32[2,128]{1,0:T(2,128)} %bitcast.24, bf16[128,3584]{1,0:T(8,128)(2,1)} %tok_ref.1, bf16[128,896]{1,0:T(8,128)(2,1)} %cot_ref.3), custom_call_target="tpu_custom_call" | custom-call | flops 1000 | bytes 1000 | tf_op jit(solution)/shard_map/pallas_call | solution.py:125
  4.2 30.1 %all_to_all.20 = bf16[32,8,1152]{2,1,0:T(8,128)(2,1)S(1)} all-to-all(bf16[32,8,1152]{2,1,0:T(8,128)(2,1)} %bitcast.31), channel_id=1, replica_groups=mesh['dp'=4,'group'=2,'expert'=32] {'expert'}, dimensions={0} | all-to-all | bytes 1179648 | tf_op jit(solution)/shard_map/all_to_all | solution.py:405
  34.3 0.5 collective-permute-start.1
  34.8 1.5 collective-permute-start
  36.3 5.9 %all-to-all-start.1 = ((bf16[32,8,1152]{2,1,0:T(8,128)(2,1)}), bf16[32,8,1152]{2,1,0:T(8,128)(2,1)S(1)}, u32[]{:S(2)}, u32[]{:S(2)}) async-start(bf16[32,8,1152]{2,1,0:T(8,128)(2,1)} %bitcast.30), calls=%async_computation.1 | async-start | bytes 1179648 | tf_op jit(solution)/shard_map/all_to_all | solution.py:405
  42.2 4.7 %collective-permute-done.1.low._ = bf16[256,1152]{1,0:T(8,128)(2,1)S(1)} collective-permute-done((bf16[256,1152]{1,0:T(8,128)(2,1)S(1)}, bf16[256,1152]{1,0:T(8,128)(2,1)S(1)}, u32[]{:S(2)}, u32[]{:S(2)}) %collective-permute-start.1) | collective-permute-done | bytes 589856 | tf_op jit(solution)/shard_map/ppermute | solution.py:351
  46.9 1.4 collective-permute-done.high
  48.4 0.4 collective-permute-start.2
  48.7 1.7 %collective-permute-start.3 = (bf16[128,1152]{1,0:T(8,128)(2,1)S(1)}, bf16[128,1152]{1,0:T(8,128)(2,1)S(1)}, u32[]{:S(2)}, u32[]{:S(2)}) collective-permute-start(bf16[128,1152]{1,0:T(8,128)(2,1)S(1)} %get-tuple-element.44), channel_id=1, source_target_pairs={{0,192},{64,0},{128,64},{192,128},{1,193},{65,1},{129,65},{193,129... | collective-permute-start | bytes 884744 | tf_op jit(solution)/shard_map/ppermute | solution.py:351
  50.5 0.0 collective-permute-done.4.wg1
  50.5 6.5 %shard_map.96.sums = f32[2,320,768]{2,1,0:T(8,128)S(1)} custom-call(s32[1]{0:T(128)} %bitcast.2.d_ref, bf16[256,1152]{1,0:T(8,128)(2,1)S(1)} %bitcast.21, bf16[256,1152]{1,0:T(8,128)(2,1)S(1)} %collective-permute-done.high, bf16[256,1152]{1,0:T(8,128)(2,1)S(1)} %collective-permute-done.1.low._, bf16[3584,384]{1,0:T(8,128)(2,1)} %bitcast.27, ...), custom_call_target="tpu_custom_call" | custom-call | flops 6000000000 | bytes 1000 | tf_op jit(solution)/shard_map/pallas_call | solution.py:284
  57.0 1.3 copy-done.3
  58.3 0.0 collective-permute-done.2.far_a
  58.3 0.0 collective-permute-done.3.far_b
  58.3 1.8 %all-to-all-done.1 = bf16[32,8,1152]{2,1,0:T(8,128)(2,1)S(1)} async-done(((bf16[32,8,1152]{2,1,0:T(8,128)(2,1)}), bf16[32,8,1152]{2,1,0:T(8,128)(2,1)S(1)}, u32[]{:S(2)}, u32[]{:S(2)}) %all-to-all-start.1) | async-done | bytes 589856 | tf_op jit(solution)/shard_map/all_to_all | solution.py:405
  60.2 0.8 collective-permute-start.8
  61.0 2.4 %collective-permute-start.9 = (bf16[256,1152]{1,0:T(8,128)(2,1)S(1)}, bf16[256,1152]{1,0:T(8,128)(2,1)S(1)}, u32[]{:S(2)}, u32[]{:S(2)}) collective-permute-start(bf16[256,1152]{1,0:T(8,128)(2,1)S(1)} %bitcast.17), channel_id=1, source_target_pairs={{0,64},{64,128},{128,192},{192,0},{1,65},{65,129},{129,193},{193,1... | collective-permute-start | bytes 1769480 | tf_op jit(solution)/shard_map/ppermute | solution.py:351
  63.4 0.0 collective-permute-start.7
  63.4 0.0 collective-permute-done.6.wd1
  63.4 5.4 %shard_map.97 = (f32[320,768]{1,0:T(8,128)S(1)}, f32[320,768]{1,0:T(8,128)S(1)}, bf16[320,768]{1,0:T(8,128)(2,1)S(1)}, bf16[128,1152]{1,0:T(8,128)(2,1)S(1)}, bf...) custom-call(s32[1]{0:T(128)} %bitcast.2.d_ref, ...), custom_call_target="tpu_custom_call" | custom-call | flops 6000000000 | bytes 1000 | tf_op jit(solution)/shard_map/pallas_call | solution.py:284
  68.9 0.6 collective-permute-start.10
  69.4 1.5 collective-permute-start.11
  71.0 3.9 %shard_map.99 = (bf16[256,1152]{1,0:T(8,128)(2,1)S(1)}, bf16[256,1152]{1,0:T(8,128)(2,1)S(1)}, bf16[256,1152]{1,0:T(8,128)(2,1)S(1)}, bf16[3,896,768]{2,1,0:T(8,128)(2,1)S(1)}) custom-call(s32[1]{0:T(128)} %bitcast.2.d_ref, bf16[320,768]{1,0:T(8,128)(2,1)S(1)} %get-tuple-element.45.h_ref, bf16[3,768,896]{2,1,0:T(8,128)(2,1)S(1)} %get-tuple-element.46.down, ...), custom_call_target="tpu_custom_call" | custom-call | flops 1000 | bytes 1000 | tf_op jit(solution)/shard_map/pallas_call | solution.py:284
  74.9 1.8 %collective-permute-start.14 = (bf16[128,1152]{1,0:T(8,128)(2,1)S(1)}, bf16[128,1152]{1,0:T(8,128)(2,1)S(1)}, u32[]{:S(2)}, u32[]{:S(2)}) collective-permute-start(bf16[128,1152]{1,0:T(8,128)(2,1)S(1)} %get-tuple-element.59), channel_id=1, source_target_pairs={{0,64},{64,128},{128,192},{192,0},{1,65},{65,129},{129,193},{193,1... | collective-permute-start | bytes 884744 | tf_op jit(solution)/shard_map/ppermute | solution.py:351
  76.7 0.3 collective-permute-start.15
  77.0 4.3 %shard_map.100 = (f32[320,768]{1,0:T(8,128)S(1)}, bf16[3,896,768]{2,1,0:T(8,128)(2,1)S(1)}) custom-call(s32[1]{0:T(128)} %bitcast.2.d_ref, bf16[256,1152]{1,0:T(8,128)(2,1)S(1)} %bitcast.18, bf16[256,1152]{1,0:T(8,128)(2,1)S(1)} %collective-permute-done.8.high, bf16[256,1152]{1,0:T(8,128)(2,1)S(1)} %collective-permute-done.9.low, ...), custom_call_target="tpu_custom_call" | custom-call | flops 6000000000 | bytes 1000 | tf_op jit(solution)/shard_map/pallas_call | solution.py:284
  81.3 0.0 collective-permute-done.10.got_a
  81.3 0.2 shard_map.101
  81.5 3.0 %collective-permute-start.12 = (bf16[256,1152]{1,0:T(8,128)(2,1)S(1)}, bf16[256,1152]{1,0:T(8,128)(2,1)S(1)}, u32[]{:S(2)}, u32[]{:S(2)}) collective-permute-start(bf16[256,1152]{1,0:T(8,128)(2,1)S(1)} %get-tuple-element.57), channel_id=1, source_target_pairs={{0,64},{64,128},{128,192},{192,0},{1,65},{65,129},{129,193},{193,1... | collective-permute-start | bytes 1769480 | tf_op jit(solution)/shard_map/ppermute | solution.py:351
  84.5 0.0 collective-permute-start.13
  84.5 0.6 collective-permute-done.14.far_a
  85.1 1.4 collective-permute-done.15.far_b
  86.5 2.8 %shard_map.104 = (bf16[320,768]{1,0:T(8,128)(2,1)S(1)}, bf16[320,768]{1,0:T(8,128)(2,1)S(1)}, bf16[128,1152]{1,0:T(8,128)(2,1)S(1)}, bf16[128,1152]{1,0:T(8,128)(2,1)S(1)}) custom-call(s32[1]{0:T(128)} %bitcast.2.d_ref, bf16[128,1152]{1,0:T(8,128)(2,1)S(1)} %collective-permute-done.14.far_a, bf16[128,1152]{1,0:T(8,128)(2,1)S(1)} %collective-permute-done.15.far_b, ...), custom_call_target="tpu_custom_call" | custom-call | flops 1000 | bytes 1000 | tf_op jit(solution)/shard_map/pallas_call | solution.py:284
  89.2 1.3 collective-permute-start.16
  90.6 0.8 collective-permute-start.17
  91.4 3.8 %shard_map.105 = (bf16[256,1152]{1,0:T(8,128)(2,1)S(1)}, bf16[256,1152]{1,0:T(8,128)(2,1)S(1)}, bf16[256,1152]{1,0:T(8,128)(2,1)S(1)}) custom-call(s32[1]{0:T(128)} %bitcast.2.d_ref, bf16[320,768]{1,0:T(8,128)(2,1)S(1)} %get-tuple-element.66.da_ref, bf16[320,768]{1,0:T(8,128)(2,1)S(1)} %get-tuple-element.67.db_ref, ...), custom_call_target="tpu_custom_call" | custom-call | flops 6000000000 | bytes 1000 | tf_op jit(solution)/shard_map/pallas_call | solution.py:284
  95.2 3.1 %collective-permute-done.12.from_low = bf16[256,1152]{1,0:T(8,128)(2,1)S(1)} collective-permute-done((bf16[256,1152]{1,0:T(8,128)(2,1)S(1)}, bf16[256,1152]{1,0:T(8,128)(2,1)S(1)}, u32[]{:S(2)}, u32[]{:S(2)}) %collective-permute-start.12) | collective-permute-done | bytes 589856 | tf_op jit(solution)/shard_map/ppermute | solution.py:351
  98.2 3.7 %collective-permute-done.13.from_high = bf16[256,1152]{1,0:T(8,128)(2,1)S(1)} collective-permute-done((bf16[256,1152]{1,0:T(8,128)(2,1)S(1)}, bf16[256,1152]{1,0:T(8,128)(2,1)S(1)}, u32[]{:S(2)}, u32[]{:S(2)}) %collective-permute-start.13) | collective-permute-done | bytes 589856 | tf_op jit(solution)/shard_map/ppermute | solution.py:351
  101.9 1.0 shard_map.102
  103.0 0.6 collective-permute-done.16.got_a
  103.6 2.7 %collective-permute-done.17.got_b = bf16[128,1152]{1,0:T(8,128)(2,1)S(1)} collective-permute-done((bf16[128,1152]{1,0:T(8,128)(2,1)S(1)}, bf16[128,1152]{1,0:T(8,128)(2,1)S(1)}, u32[]{:S(2)}, u32[]{:S(2)}) %collective-permute-start.17) | collective-permute-done | bytes 294944 | tf_op jit(solution)/shard_map/ppermute | solution.py:351
  106.3 7.8 %all-to-all-start.2 = ((bf16[32,8,1152]{2,1,0:T(8,128)(2,1)}), bf16[32,8,1152]{2,1,0:T(8,128)(2,1)S(1)}, u32[]{:S(2)}, u32[]{:S(2)}) async-start(bf16[32,8,1152]{2,1,0:T(8,128)(2,1)} %bitcast.10), calls=%async_computation.2 | async-start | bytes 1179648 | tf_op jit(solution)/shard_map/all_to_all | solution.py:405
  114.1 0.0 copy-start
  114.2 0.0 copy-start.1
  114.2 0.0 copy-start.2
  114.2 0.2 shard_map.107
  114.4 1.6 collective-permute-start.18
  115.9 0.5 collective-permute-start.19
  116.5 8.9 %collective-permute-done.18.from_low = bf16[256,1152]{1,0:T(8,128)(2,1)S(1)} collective-permute-done((bf16[256,1152]{1,0:T(8,128)(2,1)S(1)}, bf16[256,1152]{1,0:T(8,128)(2,1)S(1)}, u32[]{:S(2)}, u32[]{:S(2)}) %collective-permute-start.18) | collective-permute-done | bytes 589856 | tf_op jit(solution)/shard_map/ppermute | solution.py:351
  125.4 3.4 %collective-permute-done.19.from_high = bf16[256,1152]{1,0:T(8,128)(2,1)S(1)} collective-permute-done((bf16[256,1152]{1,0:T(8,128)(2,1)S(1)}, bf16[256,1152]{1,0:T(8,128)(2,1)S(1)}, u32[]{:S(2)}, u32[]{:S(2)}) %collective-permute-start.19) | collective-permute-done | bytes 589856 | tf_op jit(solution)/shard_map/ppermute | solution.py:351
  128.8 1.1 shard_map.108
  129.9 9.5 %all-to-all-start.3 = ((bf16[32,8,1152]{2,1,0:T(8,128)(2,1)}), bf16[32,8,1152]{2,1,0:T(8,128)(2,1)S(1)}, u32[]{:S(2)}, u32[]{:S(2)}) async-start(bf16[32,8,1152]{2,1,0:T(8,128)(2,1)} %bitcast.12), calls=%async_computation.3 | async-start | bytes 1179648 | tf_op jit(solution)/shard_map/all_to_all | solution.py:405
  139.4 1.5 shard_map.106
  141.0 0.0 collective-permute-start.20
  141.0 1.7 %collective-permute-start.21 = (f32[128,2]{1,0:T(8,128)S(1)}, f32[128,2]{1,0:T(8,128)S(1)}, u32[]{:S(2)}, u32[]{:S(2)}) collective-permute-start(f32[128,2]{1,0:T(8,128)S(1)} %get-tuple-element.80), channel_id=1, source_target_pairs={{0,64},{64,128},{128,192},{192,0},{1,65},{65,129},{129,193},{193,1... | collective-permute-start | bytes 3080 | tf_op jit(solution)/shard_map/ppermute | solution.py:351
  142.7 0.3 collective-permute-start.22
  143.0 3.7 %collective-permute-done.20 = f32[128,2]{1,0:T(8,128)S(1)} collective-permute-done((f32[128,2]{1,0:T(8,128)S(1)}, f32[128,2]{1,0:T(8,128)S(1)}, u32[]{:S(2)}, u32[]{:S(2)}) %collective-permute-start.20) | collective-permute-done | bytes 1056 | tf_op jit(solution)/shard_map/ppermute | solution.py:351
  146.7 1.4 collective-permute-done.22
  148.2 0.6 copy.10
  148.8 5.9 %all-to-all-done.3 = bf16[32,8,1152]{2,1,0:T(8,128)(2,1)S(1)} async-done(((bf16[32,8,1152]{2,1,0:T(8,128)(2,1)}), bf16[32,8,1152]{2,1,0:T(8,128)(2,1)S(1)}, u32[]{:S(2)}, u32[]{:S(2)}) %all-to-all-start.3) | async-done | bytes 589856 | tf_op jit(solution)/shard_map/all_to_all | solution.py:405
  154.7 1.1 shard_map.109
  (15 shorter events, 0.1 us)
Async XLA Ops:
  0.6 49.8 %collective-permute-start.4 = (bf16[3584,384]{1,0:T(8,128)(2,1)}, bf16[3584,384]{1,0:T(8,128)(2,1)}, u32[]{:S(2)}, u32[]{:S(2)}) collective-permute-start(bf16[3584,384]{1,0:T(8,128)(2,1)} %bitcast.26), channel_id=1, source_target_pairs={{0,32},{32,0},{1,33},{33,1},{2,34},{34,2},{3,35},{35,3},{4,36},{36... | collective-permute-start | bytes 8257544 | tf_op jit(solution)/shard_map/ppermute | solution.py:414
  0.7 49.7 %collective-permute-start.5 = (bf16[3584,384]{1,0:T(8,128)(2,1)}, bf16[3584,384]{1,0:T(8,128)(2,1)}, u32[]{:S(2)}, u32[]{:S(2)}) collective-permute-start(bf16[3584,384]{1,0:T(8,128)(2,1)} %bitcast.34), channel_id=1, source_target_pairs={{0,32},{32,0},{1,33},{33,1},{2,34},{34,2},{3,35},{35,3},{4,36},{36... | collective-permute-start | bytes 8257544 | tf_op jit(solution)/shard_map/ppermute | solution.py:414
  1.2 62.2 %collective-permute-start.6 = (bf16[384,3584]{1,0:T(8,128)(2,1)}, bf16[384,3584]{1,0:T(8,128)(2,1)}, u32[]{:S(2)}, u32[]{:S(2)}) collective-permute-start(bf16[384,3584]{1,0:T(8,128)(2,1)} %bitcast.32), channel_id=1, source_target_pairs={{0,32},{32,0},{1,33},{33,1},{2,34},{34,2},{3,35},{35,3},{4,36},{36... | collective-permute-start | bytes 8257544 | tf_op jit(solution)/shard_map/ppermute | solution.py:414
  34.3 12.6 %collective-permute-start.1 = (bf16[256,1152]{1,0:T(8,128)(2,1)S(1)}, bf16[256,1152]{1,0:T(8,128)(2,1)S(1)}, u32[]{:S(2)}, u32[]{:S(2)}) collective-permute-start(bf16[256,1152]{1,0:T(8,128)(2,1)S(1)} %bitcast.19), channel_id=1, source_target_pairs={{0,64},{64,128},{128,192},{192,0},{1,65},{65,129},{129,193},{193,1... | collective-permute-start | bytes 1769480 | tf_op jit(solution)/shard_map/ppermute | solution.py:351
  34.8 13.5 %collective-permute-start = (bf16[256,1152]{1,0:T(8,128)(2,1)S(1)}, bf16[256,1152]{1,0:T(8,128)(2,1)S(1)}, u32[]{:S(2)}, u32[]{:S(2)}) collective-permute-start(bf16[256,1152]{1,0:T(8,128)(2,1)S(1)} %bitcast.20), channel_id=1, source_target_pairs={{0,192},{64,0},{128,64},{192,128},{1,193},{65,1},{129,65},{193,129... | collective-permute-start | bytes 1769480 | tf_op jit(solution)/shard_map/ppermute | solution.py:351
  36.3 23.8 %all-to-all-start.1 = ((bf16[32,8,1152]{2,1,0:T(8,128)(2,1)}), bf16[32,8,1152]{2,1,0:T(8,128)(2,1)S(1)}, u32[]{:S(2)}, u32[]{:S(2)}) async-start(bf16[32,8,1152]{2,1,0:T(8,128)(2,1)} %bitcast.30), calls=%async_computation.1 | async-start | bytes 1179648 | tf_op jit(solution)/shard_map/all_to_all | solution.py:405
  48.4 10.0 %collective-permute-start.2 = (bf16[128,1152]{1,0:T(8,128)(2,1)S(1)}, bf16[128,1152]{1,0:T(8,128)(2,1)S(1)}, u32[]{:S(2)}, u32[]{:S(2)}) collective-permute-start(bf16[128,1152]{1,0:T(8,128)(2,1)S(1)} %get-tuple-element.43), channel_id=1, source_target_pairs={{0,64},{64,128},{128,192},{192,0},{1,65},{65,129},{129,193},{193,1... | collective-permute-start | bytes 884744 | tf_op jit(solution)/shard_map/ppermute | solution.py:351
  48.7 9.6 %collective-permute-start.3 = (bf16[128,1152]{1,0:T(8,128)(2,1)S(1)}, bf16[128,1152]{1,0:T(8,128)(2,1)S(1)}, u32[]{:S(2)}, u32[]{:S(2)}) collective-permute-start(bf16[128,1152]{1,0:T(8,128)(2,1)S(1)} %get-tuple-element.44), channel_id=1, source_target_pairs={{0,192},{64,0},{128,64},{192,128},{1,193},{65,1},{129,65},{193,129... | collective-permute-start | bytes 884744 | tf_op jit(solution)/shard_map/ppermute | solution.py:351
  57.0 1.3 copy-start.3
  60.2 14.7 %collective-permute-start.8 = (bf16[256,1152]{1,0:T(8,128)(2,1)S(1)}, bf16[256,1152]{1,0:T(8,128)(2,1)S(1)}, u32[]{:S(2)}, u32[]{:S(2)}) collective-permute-start(bf16[256,1152]{1,0:T(8,128)(2,1)S(1)} %bitcast.16), channel_id=1, source_target_pairs={{0,192},{64,0},{128,64},{192,128},{1,193},{65,1},{129,65},{193,129... | collective-permute-start | bytes 1769480 | tf_op jit(solution)/shard_map/ppermute | solution.py:351
  61.0 13.9 %collective-permute-start.9 = (bf16[256,1152]{1,0:T(8,128)(2,1)S(1)}, bf16[256,1152]{1,0:T(8,128)(2,1)S(1)}, u32[]{:S(2)}, u32[]{:S(2)}) collective-permute-start(bf16[256,1152]{1,0:T(8,128)(2,1)S(1)} %bitcast.17), channel_id=1, source_target_pairs={{0,64},{64,128},{128,192},{192,0},{1,65},{65,129},{129,193},{193,1... | collective-permute-start | bytes 1769480 | tf_op jit(solution)/shard_map/ppermute | solution.py:351
  63.4 7.6 %collective-permute-start.7 = (f32[8,128]{1,0:T(8,128)S(1)}, f32[8,128]{1,0:T(8,128)S(1)}, u32[]{:S(2)}, u32[]{:S(2)}) collective-permute-start(f32[8,128]{1,0:T(8,128)S(1)} %shard_map.98), channel_id=1, source_target_pairs={{0,32},{32,0},{1,33},{33,1},{2,34},{34,2},{3,35},{35,3},{4,36},{36... | collective-permute-start | bytes 12296 | tf_op jit(solution)/shard_map/ppermute | solution.py:422
  68.9 12.4 %collective-permute-start.10 = (bf16[128,1152]{1,0:T(8,128)(2,1)S(1)}, bf16[128,1152]{1,0:T(8,128)(2,1)S(1)}, u32[]{:S(2)}, u32[]{:S(2)}) collective-permute-start(bf16[128,1152]{1,0:T(8,128)(2,1)S(1)} %get-tuple-element.55), channel_id=1, source_target_pairs={{0,64},{64,128},{128,192},{192,0},{1,65},{65,129},{129,193},{193,1... | collective-permute-start | bytes 884744 | tf_op jit(solution)/shard_map/ppermute | solution.py:351
  69.4 11.9 %collective-permute-start.11 = (bf16[128,1152]{1,0:T(8,128)(2,1)S(1)}, bf16[128,1152]{1,0:T(8,128)(2,1)S(1)}, u32[]{:S(2)}, u32[]{:S(2)}) collective-permute-start(bf16[128,1152]{1,0:T(8,128)(2,1)S(1)} %get-tuple-element.56), channel_id=1, source_target_pairs={{0,192},{64,0},{128,64},{192,128},{1,193},{65,1},{129,65},{193,129... | collective-permute-start | bytes 884744 | tf_op jit(solution)/shard_map/ppermute | solution.py:351
  74.9 10.1 %collective-permute-start.14 = (bf16[128,1152]{1,0:T(8,128)(2,1)S(1)}, bf16[128,1152]{1,0:T(8,128)(2,1)S(1)}, u32[]{:S(2)}, u32[]{:S(2)}) collective-permute-start(bf16[128,1152]{1,0:T(8,128)(2,1)S(1)} %get-tuple-element.59), channel_id=1, source_target_pairs={{0,64},{64,128},{128,192},{192,0},{1,65},{65,129},{129,193},{193,1... | collective-permute-start | bytes 884744 | tf_op jit(solution)/shard_map/ppermute | solution.py:351
  76.7 9.8 %collective-permute-start.15 = (bf16[128,1152]{1,0:T(8,128)(2,1)S(1)}, bf16[128,1152]{1,0:T(8,128)(2,1)S(1)}, u32[]{:S(2)}, u32[]{:S(2)}) collective-permute-start(bf16[128,1152]{1,0:T(8,128)(2,1)S(1)} %get-tuple-element.60), channel_id=1, source_target_pairs={{0,192},{64,0},{128,64},{192,128},{1,193},{65,1},{129,65},{193,129... | collective-permute-start | bytes 884744 | tf_op jit(solution)/shard_map/ppermute | solution.py:351
  81.5 16.8 %collective-permute-start.12 = (bf16[256,1152]{1,0:T(8,128)(2,1)S(1)}, bf16[256,1152]{1,0:T(8,128)(2,1)S(1)}, u32[]{:S(2)}, u32[]{:S(2)}) collective-permute-start(bf16[256,1152]{1,0:T(8,128)(2,1)S(1)} %get-tuple-element.57), channel_id=1, source_target_pairs={{0,64},{64,128},{128,192},{192,0},{1,65},{65,129},{129,193},{193,1... | collective-permute-start | bytes 1769480 | tf_op jit(solution)/shard_map/ppermute | solution.py:351
  84.5 17.5 %collective-permute-start.13 = (bf16[256,1152]{1,0:T(8,128)(2,1)S(1)}, bf16[256,1152]{1,0:T(8,128)(2,1)S(1)}, u32[]{:S(2)}, u32[]{:S(2)}) collective-permute-start(bf16[256,1152]{1,0:T(8,128)(2,1)S(1)} %get-tuple-element.58), channel_id=1, source_target_pairs={{0,192},{64,0},{128,64},{192,128},{1,193},{65,1},{129,65},{193,129... | collective-permute-start | bytes 1769480 | tf_op jit(solution)/shard_map/ppermute | solution.py:351
  89.2 14.4 %collective-permute-start.16 = (bf16[128,1152]{1,0:T(8,128)(2,1)S(1)}, bf16[128,1152]{1,0:T(8,128)(2,1)S(1)}, u32[]{:S(2)}, u32[]{:S(2)}) collective-permute-start(bf16[128,1152]{1,0:T(8,128)(2,1)S(1)} %get-tuple-element.71), channel_id=1, source_target_pairs={{0,64},{64,128},{128,192},{192,0},{1,65},{65,129},{129,193},{193,1... | collective-permute-start | bytes 884744 | tf_op jit(solution)/shard_map/ppermute | solution.py:351
  90.6 15.8 %collective-permute-start.17 = (bf16[128,1152]{1,0:T(8,128)(2,1)S(1)}, bf16[128,1152]{1,0:T(8,128)(2,1)S(1)}, u32[]{:S(2)}, u32[]{:S(2)}) collective-permute-start(bf16[128,1152]{1,0:T(8,128)(2,1)S(1)} %get-tuple-element.72), channel_id=1, source_target_pairs={{0,192},{64,0},{128,64},{192,128},{1,193},{65,1},{129,65},{193,129... | collective-permute-start | bytes 884744 | tf_op jit(solution)/shard_map/ppermute | solution.py:351
  106.3 23.5 %all-to-all-start.2 = ((bf16[32,8,1152]{2,1,0:T(8,128)(2,1)}), bf16[32,8,1152]{2,1,0:T(8,128)(2,1)S(1)}, u32[]{:S(2)}, u32[]{:S(2)}) async-start(bf16[32,8,1152]{2,1,0:T(8,128)(2,1)} %bitcast.10), calls=%async_computation.2 | async-start | bytes 1179648 | tf_op jit(solution)/shard_map/all_to_all | solution.py:405
  114.1 25.2 %copy-start = (bf16[128,896]{1,0:T(8,128)(2,1)S(1)}, bf16[128,896]{1,0:T(8,128)(2,1)}, u32[]{:S(2)}) copy-start(bf16[128,896]{1,0:T(8,128)(2,1)} %cot_ref.3) | copy-start | bytes 688132
  114.2 25.2 %copy-start.1 = (s32[128,2]{0,1:T(2,128)S(1)}, s32[128,2]{0,1:T(2,128)}, u32[]{:S(2)}) copy-start(s32[128,2]{0,1:T(2,128)} %param.8) | copy-start | bytes 3076
  114.2 25.2 %copy-start.2 = (f32[128,2]{0,1:T(2,128)S(1)}, f32[128,2]{0,1:T(2,128)}, u32[]{:S(2)}) copy-start(f32[128,2]{0,1:T(2,128)} %param.9) | copy-start | bytes 3076
  114.4 11.0 %collective-permute-start.18 = (bf16[256,1152]{1,0:T(8,128)(2,1)S(1)}, bf16[256,1152]{1,0:T(8,128)(2,1)S(1)}, u32[]{:S(2)}, u32[]{:S(2)}) collective-permute-start(bf16[256,1152]{1,0:T(8,128)(2,1)S(1)} %get-tuple-element.78), channel_id=1, source_target_pairs={{0,64},{64,128},{128,192},{192,0},{1,65},{65,129},{129,193},{193,1... | collective-permute-start | bytes 1769480 | tf_op jit(solution)/shard_map/ppermute | solution.py:351
  115.9 12.9 %collective-permute-start.19 = (bf16[256,1152]{1,0:T(8,128)(2,1)S(1)}, bf16[256,1152]{1,0:T(8,128)(2,1)S(1)}, u32[]{:S(2)}, u32[]{:S(2)}) collective-permute-start(bf16[256,1152]{1,0:T(8,128)(2,1)S(1)} %get-tuple-element.79), channel_id=1, source_target_pairs={{0,192},{64,0},{128,64},{192,128},{1,193},{65,1},{129,65},{193,129... | collective-permute-start | bytes 1769480 | tf_op jit(solution)/shard_map/ppermute | solution.py:351
  129.9 24.8 %all-to-all-start.3 = ((bf16[32,8,1152]{2,1,0:T(8,128)(2,1)}), bf16[32,8,1152]{2,1,0:T(8,128)(2,1)S(1)}, u32[]{:S(2)}, u32[]{:S(2)}) async-start(bf16[32,8,1152]{2,1,0:T(8,128)(2,1)} %bitcast.12), calls=%async_computation.3 | async-start | bytes 1179648 | tf_op jit(solution)/shard_map/all_to_all | solution.py:405
  141.0 5.8 %collective-permute-start.20 = (f32[128,2]{1,0:T(8,128)S(1)}, f32[128,2]{1,0:T(8,128)S(1)}, u32[]{:S(2)}, u32[]{:S(2)}) collective-permute-start(f32[128,2]{1,0:T(8,128)S(1)} %get-tuple-element.80), channel_id=1, source_target_pairs={{0,128},{64,192},{128,0},{192,64},{1,129},{65,193},{129,1},{193,65... | collective-permute-start | bytes 3080 | tf_op jit(solution)/shard_map/ppermute | solution.py:351
  141.0 5.8 %collective-permute-start.21 = (f32[128,2]{1,0:T(8,128)S(1)}, f32[128,2]{1,0:T(8,128)S(1)}, u32[]{:S(2)}, u32[]{:S(2)}) collective-permute-start(f32[128,2]{1,0:T(8,128)S(1)} %get-tuple-element.80), channel_id=1, source_target_pairs={{0,64},{64,128},{128,192},{192,0},{1,65},{65,129},{129,193},{193,1... | collective-permute-start | bytes 3080 | tf_op jit(solution)/shard_map/ppermute | solution.py:351
  142.7 5.5 %collective-permute-start.22 = (f32[128,2]{1,0:T(8,128)S(1)}, f32[128,2]{1,0:T(8,128)S(1)}, u32[]{:S(2)}, u32[]{:S(2)}) collective-permute-start(f32[128,2]{1,0:T(8,128)S(1)} %get-tuple-element.80), channel_id=1, source_target_pairs={{0,192},{64,0},{128,64},{192,128},{1,193},{65,1},{129,65},{193,129... | collective-permute-start | bytes 3080 | tf_op jit(solution)/shard_map/ppermute | solution.py:351
